TPU v7x, 128 devices: a whole 4x4x4 slice. The times are simulated.
128 devices in a mesh: win: 32 (over x, z, core), rep: 4 (over y).
Axes of the slice: x: 4, y: 4, z: 4, core: 2. Of those that a mesh axis runs over, the one named last changes fastest.
Arguments:
- events: bfloat16 [32, 4, 256, 768], P('win', 'rep'), may hold values from -8 to 8
- send_counts: int32 [32, 4, 32], P('win', 'rep'), may hold values from 0 to 16, as said below
- patient_ids: int32 [32, 4, 256], P('win', 'rep'), may hold values from 0 to 15
- codes: int32 [32, 4, 256], P('win', 'rep'), may hold values from 0 to 4095
- event_piece: int32 [32, 4, 256], P('win', 'rep'), may hold values from 0 to 7
- censor_piece: int32 [32, 4, 256], P('win', 'rep'), may hold values from 0 to 7
- norm_gain: float32 [768], replicated, may hold values from 0.5 to 1.5
- w_qkv: bfloat16 [768, 2304], replicated, may hold values from -1 to 1
- w_out: bfloat16 [768, 768], replicated, may hold values from -0.21875 to 0.21875
- w_piece: bfloat16 [768, 1024], replicated, may hold values from -0.21875 to 0.21875
- code_table: bfloat16 [4096, 128], replicated, may hold values from -0.5 to 0.5
Outputs:
- grad_events: bfloat16 [32, 4, 256, 768], P('win', 'rep')
- grad_gain: float32 [768], P(('win', 'rep'))
- grad_qkv: float32 [768, 2304], P(('win', 'rep'))
- grad_out: float32 [768, 768], P(('win', 'rep'))
- grad_piece: float32 [768, 1024], P(('win', 'rep'))
- grad_table: float32 [4096, 128], P(('win', 'rep'))
Inputs may be any that keep to these rules, and one draw needn't show every extreme that they name: `send_counts`: every device's counts sum to 256. In every replica group one owner receives 16 events from every device, 512 in all; no owner receives more than 512.
All inputs are finite; a program needn't handle non-finite values.
Results may differ from a plain program's by a relative error of at most 0.018.
The roundings to bfloat16 on the way count: a program that leaves them out, or rounds other values in their place, can miss the bound.
Values may be sent and summed in bfloat16 or wider, within the bound.
A program may use at most 128 MiB of HBM per device.

v0:
```python
import math

import jax
import jax.numpy as jnp
from jax import lax
from jax.sharding import PartitionSpec as P

HEADS = 12


EPSILON = 1e-05


def pack_rows(source, labels, counts, slot_len):
    total_rows = source.shape[0]
    starts = jnp.cumsum(counts, dtype=jnp.int32) - counts
    offset = jnp.arange(slot_len, dtype=jnp.int32)
    take_index = jnp.clip(starts[:, None] + offset[None, :], 0, total_rows - 1)
    filled = offset[None, :] < counts[:, None]
    packed = jnp.where(filled[:, :, None], source[take_index], jnp.zeros((), source.dtype))
    packed_labels = jnp.where(filled[:, :, None], labels[take_index], 0)
    return (packed, packed_labels)


def unpack_rows(returned, counts, total_rows):
    slot_len = returned.shape[1]
    sources = counts.shape[0]
    ends_at = jnp.cumsum(counts, dtype=jnp.int32)
    starts = ends_at - counts
    position = jnp.arange(total_rows, dtype=jnp.int32)
    owner_of = jnp.minimum(
        jnp.sum((ends_at[None, :] <= position[:, None]).astype(jnp.int32), 1, dtype=jnp.int32),
        sources - 1,
    )
    chosen = owner_of[:, None] == jnp.arange(sources, dtype=jnp.int32)[None, :]
    first_slot = jnp.sum(jnp.where(chosen, starts[None, :], 0), 1, dtype=jnp.int32)
    flat_index = owner_of * slot_len + position - first_slot
    return returned.reshape(-1, returned.shape[2])[flat_index]


def compact(received, received_labels, counts, block_len):
    sources, slot_len, row_width = received.shape
    ends_at = jnp.cumsum(counts, dtype=jnp.int32)
    starts = ends_at - counts
    position = jnp.arange(block_len, dtype=jnp.int32)
    source_of = jnp.minimum(
        jnp.sum((ends_at[None, :] <= position[:, None]).astype(jnp.int32), 1, dtype=jnp.int32),
        sources - 1,
    )
    chosen = source_of[:, None] == jnp.arange(sources, dtype=jnp.int32)[None, :]
    first_slot = jnp.sum(jnp.where(chosen, starts[None, :], 0), 1, dtype=jnp.int32)
    is_valid = position < ends_at[-1]
    flat_index = jnp.clip(source_of * slot_len + position - first_slot, 0, sources * slot_len - 1)
    event_block = jnp.where(
        is_valid[:, None],
        received.reshape(-1, row_width)[flat_index],
        jnp.zeros((), received.dtype),
    )
    labels = received_labels.reshape(-1, received_labels.shape[2])[flat_index]
    return (event_block, labels, is_valid, starts)


def uncompact(grad_block, starts, counts, slot_len):
    block_len = grad_block.shape[0]
    offset = jnp.arange(slot_len, dtype=jnp.int32)
    take_index = jnp.clip(starts[:, None] + offset[None, :], 0, block_len - 1).astype(jnp.int32)
    filled = offset[None, :] < counts[:, None]
    return jnp.where(filled[:, :, None], grad_block[take_index], jnp.zeros((), grad_block.dtype))


def softmax_rows(query_head, key_head, allowed, score_scale):
    scores = jnp.dot(query_head, key_head.T, preferred_element_type=jnp.float32) * score_scale
    masked = jnp.where(allowed, scores, -1e30)
    row_max = jnp.max(masked, -1, keepdims=True)
    weights = jnp.where(allowed, jnp.exp(masked - row_max), 0.0)
    return weights / jnp.sum(weights, -1, keepdims=True)


def layer_forward(event_block, patient, norm_gain, w_qkv, w_out):
    block_len, row_width = event_block.shape
    head_dim = row_width // HEADS
    score_scale = 1.0 / math.sqrt(head_dim)
    x_float = event_block.astype(jnp.float32)
    mean_sq = jnp.mean(x_float * x_float, -1, keepdims=True)
    inv_rms = lax.rsqrt(mean_sq + EPSILON)
    x_hat = x_float * inv_rms
    normed = (x_hat * norm_gain).astype(jnp.bfloat16)
    qkv_all = jnp.dot(normed, w_qkv, preferred_element_type=jnp.float32).astype(jnp.bfloat16)
    per_head = qkv_all.reshape(block_len, 3, HEADS, head_dim).transpose(1, 2, 0, 3)
    position = jnp.arange(block_len, dtype=jnp.int32)
    allowed = (patient[:, None] == patient[None, :]) & (position[None, :] <= position[:, None]) | (
        position[:, None] == position[None, :]
    )

    def attend(head_inputs):
        query_head, key_head, values = head_inputs
        prob_rows = softmax_rows(query_head, key_head, allowed, score_scale).astype(jnp.bfloat16)
        return jnp.dot(prob_rows, values, preferred_element_type=jnp.float32).astype(jnp.bfloat16)

    context_heads = lax.map(attend, (per_head[0], per_head[1], per_head[2]))
    context = context_heads.transpose(1, 0, 2).reshape(block_len, row_width)
    attn_out = jnp.dot(context, w_out, preferred_element_type=jnp.float32)
    hidden = (x_float + attn_out).astype(jnp.bfloat16)
    return (hidden, (x_hat, inv_rms, normed, per_head, context, allowed))


def layer_backward(grad_hidden, saved_state, norm_gain, w_qkv, w_out):
    x_hat, inv_rms, normed, per_head, context, allowed = saved_state
    block_len, row_width = grad_hidden.shape
    head_dim = row_width // HEADS
    score_scale = 1.0 / math.sqrt(head_dim)
    grad_wout = jnp.dot(context.T, grad_hidden, preferred_element_type=jnp.float32)
    grad_context = jnp.dot(grad_hidden, w_out.T, preferred_element_type=jnp.float32).astype(
        jnp.bfloat16
    )
    grad_heads = grad_context.reshape(block_len, HEADS, head_dim).transpose(1, 0, 2)

    def backward_head(head_inputs):
        query_head, key_head, values, upstream = head_inputs
        prob_rows = softmax_rows(query_head, key_head, allowed, score_scale)
        prob_low = prob_rows.astype(jnp.bfloat16)
        grad_probs = jnp.dot(upstream, values.T, preferred_element_type=jnp.float32)
        grad_values = jnp.dot(prob_low.T, upstream, preferred_element_type=jnp.float32)
        inner_sum = jnp.sum(grad_probs * prob_rows, -1, keepdims=True)
        grad_scores = (prob_rows * (grad_probs - inner_sum) * score_scale).astype(jnp.bfloat16)
        grad_query = jnp.dot(grad_scores, key_head, preferred_element_type=jnp.float32)
        grad_keys = jnp.dot(grad_scores.T, query_head, preferred_element_type=jnp.float32)
        return jnp.stack([grad_query, grad_keys, grad_values])

    stacked = lax.map(backward_head, (per_head[0], per_head[1], per_head[2], grad_heads))
    grad_qkv_rows = (
        stacked.transpose(2, 1, 0, 3).reshape(block_len, 3 * row_width).astype(jnp.bfloat16)
    )
    grad_wqkv = jnp.dot(normed.T, grad_qkv_rows, preferred_element_type=jnp.float32)
    grad_normed = jnp.dot(grad_qkv_rows, w_qkv.T, preferred_element_type=jnp.float32)
    grad_gain = jnp.sum(grad_normed * x_hat, 0)
    grad_hat = grad_normed * norm_gain
    grad_float = inv_rms * (grad_hat - x_hat * jnp.mean(grad_hat * x_hat, -1, keepdims=True))
    grad_block = (grad_float + grad_hidden.astype(jnp.float32)).astype(jnp.bfloat16)
    return (grad_block, grad_gain, grad_wqkv, grad_wout)


def hazard_rows(piece_reps, is_valid, target_code, event_ids, end_ids, code_table):
    row_count = piece_reps.shape[0]
    codes_total, rep_width = code_table.shape
    pieces_total = piece_reps.shape[1] // rep_width
    piece_stack = piece_reps.reshape(row_count, pieces_total, rep_width).transpose(1, 0, 2)
    code_ids = jnp.arange(codes_total, dtype=jnp.int32)
    is_code = target_code[:, None] == code_ids[None, :]
    last_piece = jnp.where(is_code, event_ids[:, None], end_ids[:, None])
    log_codes = math.log(codes_total)

    def one_piece(running, piece_inputs):
        reps_now, piece_index = piece_inputs
        logits = jnp.dot(reps_now, code_table.T, preferred_element_type=jnp.float32) - log_codes
        live_mask = (piece_index <= last_piece) & is_valid[:, None]
        target = is_code & (event_ids[:, None] == piece_index) & is_valid[:, None]
        grad_logits = (
            jnp.where(live_mask, jnp.exp(logits), 0.0) - target.astype(jnp.float32)
        ).astype(jnp.bfloat16)
        running = running + jnp.dot(grad_logits.T, reps_now, preferred_element_type=jnp.float32)
        return (running, jnp.dot(grad_logits, code_table, preferred_element_type=jnp.float32))

    zero_table = jnp.zeros((codes_total, rep_width), jnp.float32)
    grad_table, grad_stack = lax.scan(
        one_piece, zero_table, (piece_stack, jnp.arange(pieces_total, dtype=jnp.int32))
    )
    grad_reps = grad_stack.transpose(1, 0, 2).reshape(row_count, pieces_total * rep_width)
    return (grad_reps, grad_table)


def owner_step(
    received, received_labels, counts_in, block_len, norm_gain, w_qkv, w_out, w_piece, code_table
):
    event_block, labels, is_valid, starts = compact(received, received_labels, counts_in, block_len)
    patient = jnp.where(is_valid, labels[:, 0], -1)
    hidden, saved_state = layer_forward(event_block, patient, norm_gain, w_qkv, w_out)
    piece_reps = jnp.dot(hidden, w_piece, preferred_element_type=jnp.float32).astype(jnp.bfloat16)
    grad_reps, grad_table = hazard_rows(
        piece_reps, is_valid, labels[:, 1], labels[:, 2], labels[:, 3], code_table
    )
    grad_low = grad_reps.astype(jnp.bfloat16)
    grad_wpiece = jnp.dot(hidden.T, grad_low, preferred_element_type=jnp.float32)
    grad_hidden = jnp.dot(grad_low, w_piece.T, preferred_element_type=jnp.float32).astype(
        jnp.bfloat16
    )
    grad_block, grad_gain, grad_wqkv, grad_wout = layer_backward(
        grad_hidden, saved_state, norm_gain, w_qkv, w_out
    )
    grad_slots = uncompact(grad_block, starts, counts_in, received.shape[1])
    return (grad_slots, (grad_gain, grad_wqkv, grad_wout, grad_wpiece, grad_table))


def body(
    events,
    send_counts,
    patient_ids,
    codes,
    event_piece,
    censor_piece,
    norm_gain,
    w_qkv,
    w_out,
    w_piece,
    code_table,
):
    local_rows = events[0, 0]
    counts_out = send_counts[0, 0]
    windows = lax.axis_size("win")
    replicas = lax.axis_size("rep")
    total_rows = local_rows.shape[0]
    block_len = 2 * total_rows
    slot_len = block_len // windows
    end_piece = jnp.maximum(event_piece[0, 0], censor_piece[0, 0])
    labels = jnp.stack([patient_ids[0, 0], codes[0, 0], event_piece[0, 0], end_piece], -1)
    packed, packed_labels = pack_rows(local_rows, labels, counts_out, slot_len)
    received, received_labels, counts_in = (
        lax.all_to_all(packed, "win", split_axis=0, concat_axis=0, tiled=True),
        lax.all_to_all(packed_labels, "win", split_axis=0, concat_axis=0, tiled=True),
        lax.all_to_all(counts_out[:, None], "win", split_axis=0, concat_axis=0, tiled=True),
    )
    grad_slots, weight_grads = owner_step(
        received,
        received_labels,
        counts_in[:, 0],
        block_len,
        norm_gain,
        w_qkv,
        w_out,
        w_piece,
        code_table,
    )
    returned = lax.all_to_all(grad_slots, "win", split_axis=0, concat_axis=0, tiled=True)
    grad_rows = unpack_rows(returned, counts_out, total_rows)
    grad_gain, grad_wqkv, grad_wout, grad_wpiece, grad_table = weight_grads
    summed = (
        lax.psum_scatter(grad_gain, ("win", "rep"), scatter_dimension=0, tiled=True),
        lax.psum_scatter(grad_wqkv, ("win", "rep"), scatter_dimension=0, tiled=True),
        lax.psum_scatter(grad_wout, ("win", "rep"), scatter_dimension=0, tiled=True),
        lax.psum_scatter(grad_wpiece, ("win", "rep"), scatter_dimension=0, tiled=True),
        lax.psum_scatter(grad_table, ("win", "rep"), scatter_dimension=0, tiled=True),
    )
    factor = 1.0 / math.sqrt(total_rows * windows * replicas)
    return (
        grad_rows[None, None],
        summed[0] * factor,
        summed[1] * factor,
        summed[2] * factor,
        summed[3] * factor,
        summed[4] * factor,
    )


def solution(mesh):
    return jax.shard_map(
        body,
        mesh=mesh,
        in_specs=(
            P("win", "rep", None, None),
            P("win", "rep", None),
            P("win", "rep", None),
            P("win", "rep", None),
            P("win", "rep", None),
            P("win", "rep", None),
            P(),
            P(),
            P(),
            P(),
            P(),
        ),
        out_specs=(
            P("win", "rep", None, None),
            P(("win", "rep")),
            P(("win", "rep"), None),
            P(("win", "rep"), None),
            P(("win", "rep"), None),
            P(("win", "rep"), None),
        ),
        check_vma=False,
    )
```

profile of v0, /device:TPU:0, one launch (start us, length us, event | category | flops | bytes accessed | tf_op | source)
XLA Modules:
  0.0 1301.6 jit_solution(3456581754417021246)
XLA Ops:
  8.7 8.4 all-to-all-start
  25.4 4.1 gather_fusion
  37.6 7.4 all-to-all-start.2
  52.5 6.9 all-to-all-start.1
  69.3 3.9 all-to-all-done.1
  73.3 4.5 gather_fusion.1
  79.9 4.7 convolution_convert_fusion.1
  84.6 4.3 copy.84
  99.4 42.5 %while.39 = (s32[]{:T(128)}, bf16[12,512,64]{1,2,0:T(8,128)(2,1)}, bf16[12,512,64]{2,1,0:T(8,128)(2,1)}, bf16[12,512,64]{2,1,0:T(8,128)(2,1)}, bf16[12,512,64]{2...) while((s32[]{:T(128)}, bf16[12,512,64]{1,2,0:T(8,128)(2,1)}, ...), condition=%wide.region_8.9_spmd.clone, body=%wide.region_5.8_spmd.clone.sunk | while | flops 73694208 | bytes 3629149 | solution.py:100
  147.2 152.2 %while.41 = (s32[]{:T(128)}, f32[4096,128]{1,0:T(8,128)}, bf16[8,512,128]{1,2,0:T(8,128)(2,1)}, s32[8]{0:T(128)}, bf16[8,512,128]{2,1,0:T(8,128)(2,1)}, /*index=...) while((s32[]{:T(128)}, f32[4096,128]{1,0:T(8,128)}, ...), condition=%wide.region_10.11_spmd.clone.clone.clone, body=%wide.region_9.10_spmd.clone.clone.clone.sunk | while | flops 1634731008 | bytes 40381156 | solution.py:165
  150.4 8.6 subtract_convert_fusion.2
  159.0 4.9 convolution_add_fusion.2
  168.7 8.6 subtract_convert_fusion.2
  177.3 5.6 convolution_add_fusion.2
  187.8 8.6 subtract_convert_fusion.2
  196.4 5.6 convolution_add_fusion.2
  206.8 8.6 subtract_convert_fusion.2
  215.4 5.6 convolution_add_fusion.2
  225.9 8.6 subtract_convert_fusion.2
  234.5 5.6 convolution_add_fusion.2
  244.9 8.6 subtract_convert_fusion.2
  253.5 5.6 convolution_add_fusion.2
  264.0 8.6 subtract_convert_fusion.2
  272.6 5.6 convolution_add_fusion.2
  283.0 8.6 subtract_convert_fusion.2
  291.6 5.6 convolution_add_fusion.2
  311.2 91.9 %while.40 = (s32[]{:T(128)}, bf16[12,3,512,64]{2,3,0,1:T(8,128)(2,1)}, bf16[12,512,64]{2,1,0:T(8,128)(2,1)}, bf16[12,512,64]{2,1,0:T(8,128)(2,1)}, bf16[12,512,6...) while((s32[]{:T(128)}, ...), condition=%wide.region_15.16_spmd.clone, body=%wide.region_11.15_spmd.clone.sunk | while | flops 180681216 | bytes 10334325 | solution.py:130
  403.1 7.2 fusion.81
  410.4 368.0 %fusion.84 = (f32[8,2304]{1,0:T(8,128)}, f32[8,768]{1,0:T(8,128)}, f32[8,1024]{1,0:T(8,128)}) fusion(f32[768,2304]{1,0:T(8,128)} %fusion.81, f32[768,768]{1,0:T(8,128)} %fusion.87, f32[768,1024]{1,0:T(8,128)} %fusion.88), kind=kCustom, calls=%all-reduce-scatter.3 | all-reduce-scatter fusion | flops 4194305 | bytes 12713984
  796.1 9.0 collective-permute-start.54
  853.7 4.3 collective-permute-start.34
  876.6 5.5 collective-permute-start.89
  937.5 4.9 fusion.77
  969.0 4.5 gather_fusion.4
  988.0 4.6 all-to-all-start.3
  992.7 5.4 collective-permute-start.19
  998.1 5.5 collective-permute-start.18
  1003.6 4.2 collective-permute-start.17
  1007.8 4.7 collective-permute-start.16
  1012.5 4.6 collective-permute-start.15
  1017.1 62.7 %all-reduce = f32[768]{0:T(1024)S(1)} all-reduce(f32[768]{0:T(1024)S(1)} %copy-done.43), channel_id=2, replica_groups=mesh['win'=32,'rep'=4] {'win','rep'}, use_global_device_ids=true, to_apply=%region_20.21.clone | all-reduce | flops 768 | bytes 6144
  1082.9 4.7 collective-permute-start.13
  1094.2 6.9 collective-permute-start.10
  1101.7 47.0 %concatenate.1 = f32[262,768]{1,0:T(8,128)} concatenate(f32[6,768]{1,0:T(8,128)} %copy-done.28, f32[8,768]{1,0:T(8,128)} %collective-permute-done.62, f32[8,768]{1,0:T(8,128)} %collective-permute-done.61, f32[8,768]{1,0:T(8,128)} %collective-permute-done.60, f32[8,768]{1,0:T(8,128)} %collective-permute-done.59, f32[8,768]{1,0:T(8,128)} %collective-permute-done.58, ...), dimensions={0} | concatenate | bytes 1609728
  1158.0 6.4 collective-permute-start.6
  1168.9 47.8 %concatenate.2 = f32[262,1024]{1,0:T(8,128)} concatenate(f32[6,1024]{1,0:T(8,128)} %collective-permute-done.95, f32[8,1024]{1,0:T(8,128)} %collective-permute-done.94, f32[8,1024]{1,0:T(8,128)} %collective-permute-done.93, f32[8,1024]{1,0:T(8,128)} %collective-permute-done.92, f32[8,1024]{1,0:T(8,128)} %collective-permute-done.91, f32[8,1024]{1,0:T(8,128)} %collective-permute-done.90, ...), dimensions={0} | concatenate | bytes 2146304
  1220.7 6.4 collective-permute-start.2
  1234.1 54.2 %concatenate = f32[262,2304]{1,0:T(8,128)} concatenate(f32[6,2304]{1,0:T(8,128)} %copy-done.12, f32[8,2304]{1,0:T(8,128)} %collective-permute-done.30, f32[8,2304]{1,0:T(8,128)} %collective-permute-done.29, f32[8,2304]{1,0:T(8,128)} %collective-permute-done.28, f32[8,2304]{1,0:T(8,128)} %collective-permute-done.27, f32[8,2304]{1,0:T(8,128)} %collective-permute-done.26, ...), dimensions={0} | concatenate | bytes 4829184
  (552 shorter events, 459.2 us)
Async XLA Ops:
  8.7 28.9 %all-to-all-start = ((s32[32,1,1]{2,1,0:T(1,128)}), s32[32,1,1]{2,1,0:T(1,128)}, u32[]{:S(2)}, u32[]{:S(2)}) async-start(s32[32,1,1]{2,1,0:T(1,128)} %copy.81), calls=%async_computation | async-start | bytes 32768 | tf_op jit(solution)/shard_map/all_to_all | solution.py:220
  37.6 14.9 %all-to-all-start.2 = ((s32[32,16,4]{1,2,0:T(4,128)}), s32[32,16,4]{1,2,0:T(4,128)}, u32[]{:S(2)}, u32[]{:S(2)}) async-start(s32[32,16,4]{1,2,0:T(4,128)} %broadcast_select_fusion.3), calls=%async_computation.2 | async-start | bytes 131072 | tf_op jit(solution)/shard_map/all_to_all | solution.py:219
  52.5 20.7 %all-to-all-start.1 = ((bf16[32,16,768]{2,1,0:T(8,128)(2,1)}), bf16[32,16,768]{2,1,0:T(8,128)(2,1)}, u32[]{:S(2)}, u32[]{:S(2)}) async-start(bf16[32,16,768]{2,1,0:T(8,128)(2,1)} %broadcast_select_fusion.1), calls=%async_computation.1 | async-start | bytes 1572864 | tf_op jit(solution)/shard_map/all_to_all | solution.py:218
  59.4 1233.7 %reduce-scatter.8.cloned.1.call-start = ((), (), s32[]{:S(2)}) async-start(), calls=%async_computation.5 | async-start | bytes 2113536 | tf_op jit(solution)/shard_map/reduce_scatter | solution.py:241
  788.5 16.5 %collective-permute-start.58 = (f32[8,768]{1,0:T(8,128)}, f32[8,768]{1,0:T(8,128)}, u32[]{:S(2)}, u32[]{:S(2)}) collective-permute-start(f32[8,768]{1,0:T(8,128)} %get-tuple-element.527), channel_id=1, source_target_pairs={{0,27},{1,28},{2,29},{3,30},{4,31},{5,32},{6,33},{7,34},{8,35},{9,... | collective-permute-start | bytes 73736
  790.4 17.8 %collective-permute-start.57 = (f32[8,768]{1,0:T(8,128)}, f32[8,768]{1,0:T(8,128)}, u32[]{:S(2)}, u32[]{:S(2)}) collective-permute-start(f32[8,768]{1,0:T(8,128)} %get-tuple-element.527), channel_id=1, source_target_pairs={{0,26},{1,27},{2,28},{3,29},{4,30},{5,31},{6,32},{7,33},{8,34},{9,... | collective-permute-start | bytes 73736
  792.3 18.2 %collective-permute-start.56 = (f32[8,768]{1,0:T(8,128)}, f32[8,768]{1,0:T(8,128)}, u32[]{:S(2)}, u32[]{:S(2)}) collective-permute-start(f32[8,768]{1,0:T(8,128)} %get-tuple-element.527), channel_id=1, source_target_pairs={{0,25},{1,26},{2,27},{3,28},{4,29},{5,30},{6,31},{7,32},{8,33},{9,... | collective-permute-start | bytes 73736
  794.2 18.2 %collective-permute-start.55 = (f32[8,768]{1,0:T(8,128)}, f32[8,768]{1,0:T(8,128)}, u32[]{:S(2)}, u32[]{:S(2)}) collective-permute-start(f32[8,768]{1,0:T(8,128)} %get-tuple-element.527), channel_id=1, source_target_pairs={{0,24},{1,25},{2,26},{3,27},{4,28},{5,29},{6,30},{7,31},{8,32},{9,... | collective-permute-start | bytes 73736
  796.1 20.0 %collective-permute-start.54 = (f32[8,768]{1,0:T(8,128)}, f32[8,768]{1,0:T(8,128)}, u32[]{:S(2)}, u32[]{:S(2)}) collective-permute-start(f32[8,768]{1,0:T(8,128)} %get-tuple-element.527), channel_id=1, source_target_pairs={{0,23},{1,24},{2,25},{3,26},{4,27},{5,28},{6,29},{7,30},{8,31},{9,... | collective-permute-start | bytes 73736
  848.9 15.0 %collective-permute-start.36 = (f32[8,768]{1,0:T(8,128)}, f32[8,768]{1,0:T(8,128)S(1)}, u32[]{:S(2)}, u32[]{:S(2)}) collective-permute-start(f32[8,768]{1,0:T(8,128)} %get-tuple-element.527), channel_id=1, source_target_pairs={{0,5},{1,6},{2,7},{3,8},{4,9},{5,10},{6,11},{7,12},{8,13},{9,14},{... | collective-permute-start | bytes 73736
  866.3 15.8 %collective-permute-start.93 = (f32[8,1024]{1,0:T(8,128)}, f32[8,1024]{1,0:T(8,128)}, u32[]{:S(2)}, u32[]{:S(2)}) collective-permute-start(f32[8,1024]{1,0:T(8,128)} %get-tuple-element.528), channel_id=1, source_target_pairs={{0,30},{1,31},{2,32},{3,33},{4,34},{5,35},{6,36},{7,37},{8,38},{9,... | collective-permute-start | bytes 98312
  868.2 16.1 %collective-permute-start.92 = (f32[8,1024]{1,0:T(8,128)}, f32[8,1024]{1,0:T(8,128)}, u32[]{:S(2)}, u32[]{:S(2)}) collective-permute-start(f32[8,1024]{1,0:T(8,128)} %get-tuple-element.528), channel_id=1, source_target_pairs={{0,29},{1,30},{2,31},{3,32},{4,33},{5,34},{6,35},{7,36},{8,37},{9,... | collective-permute-start | bytes 98312
  874.6 15.4 %collective-permute-start.90 = (f32[8,1024]{1,0:T(8,128)}, f32[8,1024]{1,0:T(8,128)}, u32[]{:S(2)}, u32[]{:S(2)}) collective-permute-start(f32[8,1024]{1,0:T(8,128)} %get-tuple-element.528), channel_id=1, source_target_pairs={{0,27},{1,28},{2,29},{3,30},{4,31},{5,32},{6,33},{7,34},{8,35},{9,... | collective-permute-start | bytes 98312
  876.6 16.0 %collective-permute-start.89 = (f32[8,1024]{1,0:T(8,128)}, f32[8,1024]{1,0:T(8,128)}, u32[]{:S(2)}, u32[]{:S(2)}) collective-permute-start(f32[8,1024]{1,0:T(8,128)} %get-tuple-element.528), channel_id=1, source_target_pairs={{0,26},{1,27},{2,28},{3,29},{4,30},{5,31},{6,32},{7,33},{8,34},{9,... | collective-permute-start | bytes 98312
  924.3 19.0 %collective-permute-start.71 = (f32[8,1024]{1,0:T(8,128)}, f32[8,1024]{1,0:T(8,128)S(1)}, u32[]{:S(2)}, u32[]{:S(2)}) collective-permute-start(f32[8,1024]{1,0:T(8,128)} %get-tuple-element.528), channel_id=1, source_target_pairs={{0,8},{1,9},{2,10},{3,11},{4,12},{5,13},{6,14},{7,15},{8,16},{9,17... | collective-permute-start | bytes 98312
  926.6 19.0 %collective-permute-start.70 = (f32[8,1024]{1,0:T(8,128)}, f32[8,1024]{1,0:T(8,128)S(1)}, u32[]{:S(2)}, u32[]{:S(2)}) collective-permute-start(f32[8,1024]{1,0:T(8,128)} %get-tuple-element.528), channel_id=1, source_target_pairs={{0,7},{1,8},{2,9},{3,10},{4,11},{5,12},{6,13},{7,14},{8,15},{9,16}... | collective-permute-start | bytes 98312
  930.3 18.9 %collective-permute-start.69 = (f32[8,1024]{1,0:T(8,128)}, f32[8,1024]{1,0:T(8,128)S(1)}, u32[]{:S(2)}, u32[]{:S(2)}) collective-permute-start(f32[8,1024]{1,0:T(8,128)} %get-tuple-element.528), channel_id=1, source_target_pairs={{0,6},{1,7},{2,8},{3,9},{4,10},{5,11},{6,12},{7,13},{8,14},{9,15},... | collective-permute-start | bytes 98312
  932.1 20.2 %collective-permute-start.68 = (f32[8,1024]{1,0:T(8,128)}, f32[8,1024]{1,0:T(8,128)S(1)}, u32[]{:S(2)}, u32[]{:S(2)}) collective-permute-start(f32[8,1024]{1,0:T(8,128)} %get-tuple-element.528), channel_id=1, source_target_pairs={{0,5},{1,6},{2,7},{3,8},{4,9},{5,10},{6,11},{7,12},{8,13},{9,14},{... | collective-permute-start | bytes 98312
  935.4 19.0 %collective-permute-start.67 = (f32[8,1024]{1,0:T(8,128)}, f32[8,1024]{1,0:T(8,128)S(1)}, u32[]{:S(2)}, u32[]{:S(2)}) collective-permute-start(f32[8,1024]{1,0:T(8,128)} %get-tuple-element.528), channel_id=1, source_target_pairs={{0,4},{1,5},{2,6},{3,7},{4,8},{5,9},{6,10},{7,11},{8,12},{9,13},{1... | collective-permute-start | bytes 98312
  943.3 21.4 %collective-permute-start.30 = (f32[8,2304]{1,0:T(8,128)}, f32[8,2304]{1,0:T(8,128)}, u32[]{:S(2)}, u32[]{:S(2)}) collective-permute-start(f32[8,2304]{1,0:T(8,128)} %get-tuple-element.526), channel_id=1, source_target_pairs={{0,31},{1,32},{2,33},{3,34},{4,35},{5,36},{6,37},{7,38},{8,39},{9,... | collective-permute-start | bytes 221192
  955.8 17.8 %collective-permute-start.29 = (f32[8,2304]{1,0:T(8,128)}, f32[8,2304]{1,0:T(8,128)}, u32[]{:S(2)}, u32[]{:S(2)}) collective-permute-start(f32[8,2304]{1,0:T(8,128)} %get-tuple-element.526), channel_id=1, source_target_pairs={{0,30},{1,31},{2,32},{3,33},{4,34},{5,35},{6,36},{7,37},{8,38},{9,... | collective-permute-start | bytes 221192
  957.7 18.6 %collective-permute-start.28 = (f32[8,2304]{1,0:T(8,128)}, f32[8,2304]{1,0:T(8,128)}, u32[]{:S(2)}, u32[]{:S(2)}) collective-permute-start(f32[8,2304]{1,0:T(8,128)} %get-tuple-element.526), channel_id=1, source_target_pairs={{0,29},{1,30},{2,31},{3,32},{4,33},{5,34},{6,35},{7,36},{8,37},{9,... | collective-permute-start | bytes 221192
  959.6 18.6 %collective-permute-start.27 = (f32[8,2304]{1,0:T(8,128)}, f32[8,2304]{1,0:T(8,128)}, u32[]{:S(2)}, u32[]{:S(2)}) collective-permute-start(f32[8,2304]{1,0:T(8,128)} %get-tuple-element.526), channel_id=1, source_target_pairs={{0,28},{1,29},{2,30},{3,31},{4,32},{5,33},{6,34},{7,35},{8,36},{9,... | collective-permute-start | bytes 221192
  962.1 19.1 %collective-permute-start.26 = (f32[8,2304]{1,0:T(8,128)}, f32[8,2304]{1,0:T(8,128)}, u32[]{:S(2)}, u32[]{:S(2)}) collective-permute-start(f32[8,2304]{1,0:T(8,128)} %get-tuple-element.526), channel_id=1, source_target_pairs={{0,27},{1,28},{2,29},{3,30},{4,31},{5,32},{6,33},{7,34},{8,35},{9,... | collective-permute-start | bytes 221192
  964.7 19.2 %collective-permute-start.25 = (f32[8,2304]{1,0:T(8,128)}, f32[8,2304]{1,0:T(8,128)}, u32[]{:S(2)}, u32[]{:S(2)}) collective-permute-start(f32[8,2304]{1,0:T(8,128)} %get-tuple-element.526), channel_id=1, source_target_pairs={{0,26},{1,27},{2,28},{3,29},{4,30},{5,31},{6,32},{7,33},{8,34},{9,... | collective-permute-start | bytes 221192
  973.6 19.0 %collective-permute-start.24 = (f32[8,2304]{1,0:T(8,128)}, f32[8,2304]{1,0:T(8,128)}, u32[]{:S(2)}, u32[]{:S(2)}) collective-permute-start(f32[8,2304]{1,0:T(8,128)} %get-tuple-element.526), channel_id=1, source_target_pairs={{0,25},{1,26},{2,27},{3,28},{4,29},{5,30},{6,31},{7,32},{8,33},{9,... | collective-permute-start | bytes 221192
  976.2 21.8 %collective-permute-start.23 = (f32[8,2304]{1,0:T(8,128)}, f32[8,2304]{1,0:T(8,128)}, u32[]{:S(2)}, u32[]{:S(2)}) collective-permute-start(f32[8,2304]{1,0:T(8,128)} %get-tuple-element.526), channel_id=1, source_target_pairs={{0,24},{1,25},{2,26},{3,27},{4,28},{5,29},{6,30},{7,31},{8,32},{9,... | collective-permute-start | bytes 221192
  978.2 25.4 %collective-permute-start.22 = (f32[8,2304]{1,0:T(8,128)}, f32[8,2304]{1,0:T(8,128)}, u32[]{:S(2)}, u32[]{:S(2)}) collective-permute-start(f32[8,2304]{1,0:T(8,128)} %get-tuple-element.526), channel_id=1, source_target_pairs={{0,23},{1,24},{2,25},{3,26},{4,27},{5,28},{6,29},{7,30},{8,31},{9,... | collective-permute-start | bytes 221192
  981.3 26.5 %collective-permute-start.21 = (f32[8,2304]{1,0:T(8,128)}, f32[8,2304]{1,0:T(8,128)}, u32[]{:S(2)}, u32[]{:S(2)}) collective-permute-start(f32[8,2304]{1,0:T(8,128)} %get-tuple-element.526), channel_id=1, source_target_pairs={{0,22},{1,23},{2,24},{3,25},{4,26},{5,27},{6,28},{7,29},{8,30},{9,... | collective-permute-start | bytes 221192
  983.9 28.6 %collective-permute-start.20 = (f32[8,2304]{1,0:T(8,128)}, f32[8,2304]{1,0:T(8,128)}, u32[]{:S(2)}, u32[]{:S(2)}) collective-permute-start(f32[8,2304]{1,0:T(8,128)} %get-tuple-element.526), channel_id=1, source_target_pairs={{0,21},{1,22},{2,23},{3,24},{4,25},{5,26},{6,27},{7,28},{8,29},{9,... | collective-permute-start | bytes 221192
  988.0 301.8 %all-to-all-start.3 = ((bf16[32,16,768]{2,1,0:T(8,128)(2,1)}), bf16[32,16,768]{2,1,0:T(8,128)(2,1)}, u32[]{:S(2)}, u32[]{:S(2)}) async-start(bf16[32,16,768]{2,1,0:T(8,128)(2,1)} %broadcast_select_fusion.2), calls=%async_computation.3 | async-start | bytes 1572864 | tf_op jit(solution)/shard_map/all_to_all | solution.py:233
  992.7 87.1 %collective-permute-start.19 = (f32[8,2304]{1,0:T(8,128)}, f32[8,2304]{1,0:T(8,128)}, u32[]{:S(2)}, u32[]{:S(2)}) collective-permute-start(f32[8,2304]{1,0:T(8,128)} %get-tuple-element.526), channel_id=1, source_target_pairs={{0,20},{1,21},{2,22},{3,23},{4,24},{5,25},{6,26},{7,27},{8,28},{9,... | collective-permute-start | bytes 221192
  998.1 84.8 %collective-permute-start.18 = (f32[8,2304]{1,0:T(8,128)}, f32[8,2304]{1,0:T(8,128)}, u32[]{:S(2)}, u32[]{:S(2)}) collective-permute-start(f32[8,2304]{1,0:T(8,128)} %get-tuple-element.526), channel_id=1, source_target_pairs={{0,19},{1,20},{2,21},{3,22},{4,23},{5,24},{6,25},{7,26},{8,27},{9,... | collective-permute-start | bytes 221192
  1003.6 84.0 %collective-permute-start.17 = (f32[8,2304]{1,0:T(8,128)}, f32[8,2304]{1,0:T(8,128)}, u32[]{:S(2)}, u32[]{:S(2)}) collective-permute-start(f32[8,2304]{1,0:T(8,128)} %get-tuple-element.526), channel_id=1, source_target_pairs={{0,18},{1,19},{2,20},{3,21},{4,22},{5,23},{6,24},{7,25},{8,26},{9,... | collective-permute-start | bytes 221192
  1007.8 83.7 %collective-permute-start.16 = (f32[8,2304]{1,0:T(8,128)}, f32[8,2304]{1,0:T(8,128)}, u32[]{:S(2)}, u32[]{:S(2)}) collective-permute-start(f32[8,2304]{1,0:T(8,128)} %get-tuple-element.526), channel_id=1, source_target_pairs={{0,17},{1,18},{2,19},{3,20},{4,21},{5,22},{6,23},{7,24},{8,25},{9,... | collective-permute-start | bytes 221192
  1012.5 81.7 %collective-permute-start.15 = (f32[8,2304]{1,0:T(8,128)}, f32[8,2304]{1,0:T(8,128)}, u32[]{:S(2)}, u32[]{:S(2)}) collective-permute-start(f32[8,2304]{1,0:T(8,128)} %get-tuple-element.526), channel_id=1, source_target_pairs={{0,16},{1,17},{2,18},{3,19},{4,20},{5,21},{6,22},{7,23},{8,24},{9,... | collective-permute-start | bytes 221192
  1079.8 69.0 %collective-permute-start.14 = (f32[8,2304]{1,0:T(8,128)}, f32[8,2304]{1,0:T(8,128)}, u32[]{:S(2)}, u32[]{:S(2)}) collective-permute-start(f32[8,2304]{1,0:T(8,128)} %get-tuple-element.526), channel_id=1, source_target_pairs={{0,15},{1,16},{2,17},{3,18},{4,19},{5,20},{6,21},{7,22},{8,23},{9,... | collective-permute-start | bytes 221192
  1082.9 68.5 %collective-permute-start.13 = (f32[8,2304]{1,0:T(8,128)}, f32[8,2304]{1,0:T(8,128)}, u32[]{:S(2)}, u32[]{:S(2)}) collective-permute-start(f32[8,2304]{1,0:T(8,128)} %get-tuple-element.526), channel_id=1, source_target_pairs={{0,14},{1,15},{2,16},{3,17},{4,18},{5,19},{6,20},{7,21},{8,22},{9,... | collective-permute-start | bytes 221192
  1087.6 66.6 %collective-permute-start.12 = (f32[8,2304]{1,0:T(8,128)}, f32[8,2304]{1,0:T(8,128)}, u32[]{:S(2)}, u32[]{:S(2)}) collective-permute-start(f32[8,2304]{1,0:T(8,128)} %get-tuple-element.526), channel_id=1, source_target_pairs={{0,13},{1,14},{2,15},{3,16},{4,17},{5,18},{6,19},{7,20},{8,21},{9,... | collective-permute-start | bytes 221192
  1091.5 66.5 %collective-permute-start.11 = (f32[8,2304]{1,0:T(8,128)}, f32[8,2304]{1,0:T(8,128)}, u32[]{:S(2)}, u32[]{:S(2)}) collective-permute-start(f32[8,2304]{1,0:T(8,128)} %get-tuple-element.526), channel_id=1, source_target_pairs={{0,12},{1,13},{2,14},{3,15},{4,16},{5,17},{6,18},{7,19},{8,20},{9,... | collective-permute-start | bytes 221192
  1094.2 70.2 %collective-permute-start.10 = (f32[8,2304]{1,0:T(8,128)}, f32[8,2304]{1,0:T(8,128)}, u32[]{:S(2)}, u32[]{:S(2)}) collective-permute-start(f32[8,2304]{1,0:T(8,128)} %get-tuple-element.526), channel_id=1, source_target_pairs={{0,11},{1,12},{2,13},{3,14},{4,15},{5,16},{6,17},{7,18},{8,19},{9,... | collective-permute-start | bytes 221192
  1148.8 67.9 %collective-permute-start.9 = (f32[8,2304]{1,0:T(8,128)}, f32[8,2304]{1,0:T(8,128)}, u32[]{:S(2)}, u32[]{:S(2)}) collective-permute-start(f32[8,2304]{1,0:T(8,128)} %get-tuple-element.526), channel_id=1, source_target_pairs={{0,10},{1,11},{2,12},{3,13},{4,14},{5,15},{6,16},{7,17},{8,18},{9,... | collective-permute-start | bytes 221192
  1151.4 67.2 %collective-permute-start.8 = (f32[8,2304]{1,0:T(8,128)}, f32[8,2304]{1,0:T(8,128)}, u32[]{:S(2)}, u32[]{:S(2)}) collective-permute-start(f32[8,2304]{1,0:T(8,128)} %get-tuple-element.526), channel_id=1, source_target_pairs={{0,9},{1,10},{2,11},{3,12},{4,13},{5,14},{6,15},{7,16},{8,17},{9,1... | collective-permute-start | bytes 221192
  1154.2 66.4 %collective-permute-start.7 = (f32[8,2304]{1,0:T(8,128)}, f32[8,2304]{1,0:T(8,128)}, u32[]{:S(2)}, u32[]{:S(2)}) collective-permute-start(f32[8,2304]{1,0:T(8,128)} %get-tuple-element.526), channel_id=1, source_target_pairs={{0,8},{1,9},{2,10},{3,11},{4,12},{5,13},{6,14},{7,15},{8,16},{9,17... | collective-permute-start | bytes 221192
  1158.0 69.1 %collective-permute-start.6 = (f32[8,2304]{1,0:T(8,128)}, f32[8,2304]{1,0:T(8,128)}, u32[]{:S(2)}, u32[]{:S(2)}) collective-permute-start(f32[8,2304]{1,0:T(8,128)} %get-tuple-element.526), channel_id=1, source_target_pairs={{0,7},{1,8},{2,9},{3,10},{4,11},{5,12},{6,13},{7,14},{8,15},{9,16}... | collective-permute-start | bytes 221192
  1164.4 64.7 %collective-permute-start.5 = (f32[8,2304]{1,0:T(8,128)}, f32[8,2304]{1,0:T(8,128)}, u32[]{:S(2)}, u32[]{:S(2)}) collective-permute-start(f32[8,2304]{1,0:T(8,128)} %get-tuple-element.526), channel_id=1, source_target_pairs={{0,6},{1,7},{2,8},{3,9},{4,10},{5,11},{6,12},{7,13},{8,14},{9,15},... | collective-permute-start | bytes 221192
  1216.6 17.3 %collective-permute-start.4 = (f32[8,2304]{1,0:T(8,128)}, f32[8,2304]{1,0:T(8,128)}, u32[]{:S(2)}, u32[]{:S(2)}) collective-permute-start(f32[8,2304]{1,0:T(8,128)} %get-tuple-element.526), channel_id=1, source_target_pairs={{0,5},{1,6},{2,7},{3,8},{4,9},{5,10},{6,11},{7,12},{8,13},{9,14},{... | collective-permute-start | bytes 221192
  1218.6 15.3 %collective-permute-start.3 = (f32[8,2304]{1,0:T(8,128)}, f32[8,2304]{1,0:T(8,128)}, u32[]{:S(2)}, u32[]{:S(2)}) collective-permute-start(f32[8,2304]{1,0:T(8,128)} %get-tuple-element.526), channel_id=1, source_target_pairs={{0,4},{1,5},{2,6},{3,7},{4,8},{5,9},{6,10},{7,11},{8,12},{9,13},{1... | collective-permute-start | bytes 221192
  (118 other events, 2468.5 us)
Sparse Core Ops, SparseCore 0:
  410.5 642.7 reduce-scatter.7
where the time goes:
time: 1320 us; the launch traced here: 1300 us
  blocking collectives  431 us (33%)
  starting transfers between devices  294 us (22%)
  matrix products  275 us (21%)
  local copies, waits for them, and re-layouts  217 us (16%)
  other arithmetic  62.7 us (5%)
  between operations  15.3 us (1%)
    unnamed x2, blocking collectives  431 us
    unnamed x96, starting transfers between devices  267 us
    unnamed x108, local copies, waits for them, and re-layouts  164 us
    dot_general x8, matrix products, one_piece(): jnp.dot(reps_now, code_table.T, preferred_element_type=jnp.float32)  68.8 us
    dot_general x8, matrix products, one_piece(): jnp.dot(grad_logits.T, reps_now, preferred_element_type=jnp.float32)  44.4 us
    dot_general x24, matrix products, softmax_rows(): jnp.dot(query_head, key_head.T, preferred_element_type=jnp.float32)  32.3 us
  transfers between devices with their start and end apart: 101, of which 3 were waited for; matrix products, arithmetic and copies ran while one was open for 45% of the time, Pallas kernels for 0%

commit v1 on v0

v1 whole, which is shorter than its diff:
```python
import functools
import math

import jax
import jax.numpy as jnp
from jax import lax
from jax.experimental import pallas as pl
from jax.experimental.pallas import tpu as pltpu
from jax.sharding import PartitionSpec as P

HEADS = 12
EPSILON = 1e-05
MESH = pl.DeviceIdType.MESH

D = 768
PAIRS = 6
PIECES = 8
CODES = 4096
R = 128
ROWS = 512
EVENTS = 256
WIN = 32
SLOT = 16
LAB = 128
WIDE = D + LAB
BLOCK = 512

F32 = jnp.float32
BF16 = jnp.bfloat16

NT = (((1,), (1,)), ((), ()))
TN = (((0,), (0,)), ((), ()))


def mm(a, b):
    return jnp.dot(a, b, preferred_element_type=F32)


def mm_nt(a, b):
    return lax.dot_general(a, b, NT, preferred_element_type=F32)


def mm_tn(a, b):
    return lax.dot_general(a, b, TN, preferred_element_type=F32)


def exchange_rows(src_ref, dst_ref, send_sem, recv_sem, me):
    @pl.loop(1, WIN)
    def _(k):
        peer = lax.rem(me + k, WIN)
        pltpu.make_async_remote_copy(
            src_ref=src_ref.at[peer],
            dst_ref=dst_ref.at[me],
            send_sem=send_sem.at[k],
            recv_sem=recv_sem.at[k],
            device_id={"win": peer},
            device_id_type=MESH,
        ).start()


def wait_rows(src_ref, dst_ref, send_sem, recv_sem, me):
    @pl.loop(1, WIN)
    def _(k):
        sender = lax.rem(me + WIN - k, WIN)
        pltpu.make_async_remote_copy(
            src_ref=src_ref.at[me],
            dst_ref=dst_ref.at[sender],
            send_sem=send_sem.at[k],
            recv_sem=recv_sem.at[k],
            device_id={"win": sender},
            device_id_type=MESH,
        ).wait()


def dispatch_kernel(ev_ref, lab_ref, cnt_ref, out_ref, hot_ref, packed, landed, send_sem, recv_sem):
    me = lax.axis_index("win")
    barrier = pltpu.get_barrier_semaphore()

    @pl.loop(1, WIN)
    def _(k):
        pl.semaphore_signal(
            barrier, inc=1, device_id={"win": lax.rem(me + k, WIN)}, device_id_type=MESH
        )

    counts = cnt_ref[...].astype(F32)
    row = lax.broadcasted_iota(jnp.int32, (ROWS, WIN), 0)
    owner = lax.broadcasted_iota(jnp.int32, (ROWS, WIN), 1)
    row_owner = row // SLOT
    mine = jnp.sum(jnp.where(owner == row_owner, counts, 0.0), 1, keepdims=True)
    start = jnp.sum(jnp.where(owner < row_owner, counts, 0.0), 1, keepdims=True)
    offset = (lax.broadcasted_iota(jnp.int32, (ROWS, 1), 0) % SLOT).astype(F32)
    place = lax.broadcasted_iota(jnp.int32, (ROWS, EVENTS), 1).astype(F32)
    wanted = jnp.where(offset < mine, start + offset, -1.0)
    hot = jnp.where(place == wanted, 1.0, 0.0).astype(BF16)
    hot_ref[...] = hot
    packed[:, :, :D] = mm(hot, ev_ref[...]).astype(BF16).reshape(WIN, SLOT, D)

    lab = lab_ref[...]
    high = lab[1:2] // 64
    rows = [lab[0:1], high, lab[1:2] - high * 64, lab[2:3], jnp.maximum(lab[2:3], lab[3:4])]
    rows.append(jnp.ones((1, EVENTS), jnp.int32))
    rows.append(jnp.zeros((2, EVENTS), jnp.int32))
    table = jnp.concatenate(rows, 0).astype(F32)
    table = jnp.concatenate([table, jnp.zeros((LAB - 8, EVENTS), F32)], 0).astype(BF16)
    packed[:, :, D:] = mm_nt(hot, table).astype(BF16).reshape(WIN, SLOT, LAB)

    pl.semaphore_wait(barrier, WIN - 1)
    exchange_rows(packed, landed, send_sem, recv_sem, me)
    landed[me] = packed[me]
    wait_rows(packed, landed, send_sem, recv_sem, me)
    out_ref[...] = landed[...]


def dispatch(events, labels, counts):
    return pl.pallas_call(
        dispatch_kernel,
        out_shape=(
            jax.ShapeDtypeStruct((WIN, SLOT, WIDE), BF16),
            jax.ShapeDtypeStruct((ROWS, EVENTS), BF16),
        ),
        in_specs=[pl.BlockSpec(memory_space=pltpu.VMEM)] * 3,
        out_specs=(pl.BlockSpec(memory_space=pltpu.VMEM),) * 2,
        scratch_shapes=[
            pltpu.VMEM((WIN, SLOT, WIDE), BF16),
            pltpu.VMEM((WIN, SLOT, WIDE), BF16),
            pltpu.SemaphoreType.DMA((WIN,)),
            pltpu.SemaphoreType.DMA((WIN,)),
        ],
        compiler_params=pltpu.CompilerParams(
            collective_id=1, has_side_effects=True, vmem_limit_bytes=32 * 1024 * 1024
        ),
        name="dispatch",
    )(events, labels, counts)


def stack_halves(res):
    tiles = res.reshape(WIN, 3, 8, 256)
    both = jnp.concatenate([tiles[..., :128], tiles[..., 128:]], 2)
    return both.reshape(WIN, 48, 128).astype(BF16)


def lanes(index):
    return pl.ds(pl.multiple_of(index * 128, 128), 128)


def owner_kernel(
    x_ref,
    gain_ref,
    wqkv_ref,
    wout_ref,
    wpiece_ref,
    table_ref,
    gb_ref,
    sq_ref,
    so_ref,
    sp_ref,
    st_ref,
    sg_ref,
    normed,
    normed_t,
    qkv,
    prob,
    ctx,
    hidden,
    reps,
    reps_t,
    greps,
    glow,
    ghid,
    gctx,
    dqkv,
    bias,
    labs,
    gtab_t,
    gnorm,
):
    gain = gain_ref[...]
    lab = x_ref[:, D:].astype(F32)
    valid = lab[:, 5:6] > 0.5
    patient = jnp.where(valid, lab[:, 0:1], -1.0)
    labs[0] = jnp.broadcast_to(lab[:, 1:2] * 64.0 + lab[:, 2:3], (ROWS, 128))
    labs[1] = jnp.broadcast_to(jnp.where(valid, lab[:, 3:4], -1.0), (ROWS, 128))
    labs[2] = jnp.broadcast_to(jnp.where(valid, lab[:, 4:5], -1.0), (ROWS, 128))

    lab_t = lab.T
    patient_row = jnp.where(lab_t[5:6] > 0.5, lab_t[0:1], -1.0)
    row = lax.broadcasted_iota(jnp.int32, (ROWS, ROWS), 0)
    col = lax.broadcasted_iota(jnp.int32, (ROWS, ROWS), 1)
    allowed = ((patient == patient_row) & (col <= row)) | (col == row)
    bias[...] = jnp.where(allowed, 0.0, -1e30)

    x = x_ref[:, :D].astype(F32)
    inv_rms = lax.rsqrt(jnp.mean(x * x, -1, keepdims=True) + EPSILON)
    normed[...] = (x * inv_rms * gain).astype(BF16)

    @pl.loop(0, 9)
    def _(j):
        cols = pl.ds(pl.multiple_of(j * 256, 256), 256)
        res = mm(normed[...], wqkv_ref[:, cols])
        scale = jnp.where(j < 3, 0.125, 1.0)
        res = (res * scale).astype(BF16)
        qkv[2 * j] = res[:, :128]
        qkv[2 * j + 1] = res[:, 128:]

    low_lanes = lax.broadcasted_iota(jnp.int32, (1, 128), 1) < 64

    def head_part(value, head):
        zero = jnp.zeros((), value.dtype)
        return jnp.where(low_lanes, value, zero) if head == 0 else jnp.where(low_lanes, zero, value)

    @pl.loop(0, PAIRS)
    def _(p):
        q = qkv[p]
        k = qkv[PAIRS + p]
        v = qkv[2 * PAIRS + p]
        for rb in range(2):
            rs = slice(rb * 256, rb * 256 + 256)
            n = (rb + 1) * 256
            parts = []
            for head in range(2):
                s = mm_nt(head_part(q[rs], head), k[:n]) + bias[rs, :n]
                w = jnp.exp(s - jnp.max(s, -1, keepdims=True))
                pr = (w * (1.0 / jnp.sum(w, -1, keepdims=True))).astype(BF16)
                prob[p, head, rs, :n] = pr
                parts.append(mm(pr, v[:n]))
            ctx[rs, lanes(p)] = jnp.where(low_lanes, parts[0], parts[1]).astype(BF16)

    @pl.loop(0, 3)
    def _(j):
        cols = pl.ds(pl.multiple_of(j * 256, 256), 256)
        res = mm(ctx[...], wout_ref[:, cols])
        hidden[:, cols] = (x_ref[:, cols].astype(F32) + res).astype(BF16)

    @pl.loop(0, 4)
    def _(j):
        cols = pl.ds(pl.multiple_of(j * 256, 256), 256)
        res = mm(hidden[...], wpiece_ref[:, cols])
        for i in range(2):
            part = res[:, i * 128 : i * 128 + 128]
            reps[2 * j + i] = part.astype(BF16)
            reps_t[2 * j + i] = part.T.astype(BF16)

    log_codes = math.log(CODES)
    times = BLOCK // 128

    def widen(tile):
        return jnp.concatenate([tile] * times, 1)

    greps[...] = jnp.zeros_like(greps)

    @pl.loop(0, CODES // BLOCK)
    def _(b):
        codes_at = pl.ds(pl.multiple_of(b * BLOCK, BLOCK), BLOCK)
        tab = table_ref[codes_at, :]
        ids = (b * BLOCK + lax.broadcasted_iota(jnp.int32, (1, BLOCK), 1)).astype(F32)
        gtab_t[:, codes_at] = jnp.zeros((R, BLOCK), F32)

        @pl.loop(0, PIECES)
        def _(p):
            piece = p.astype(F32)
            code, event, end = labs[0], labs[1], labs[2]
            at_row = jnp.where(end >= piece, -log_codes, -1e30)
            at_code = jnp.where(event >= piece, -log_codes, -1e30)
            target = jnp.where(event == piece, 1.0, 0.0)
            logits = mm_nt(reps[p], tab)
            is_code = widen(code) == ids
            e = jnp.exp(logits + jnp.where(is_code, widen(at_code), widen(at_row)))
            g = (e - jnp.where(is_code, widen(target), 0.0)).astype(BF16)
            greps[p] += mm(g, tab)
            gtab_t[:, codes_at] += mm(reps_t[p], g)

        st_ref[codes_at, :] = gtab_t[:, codes_at].T.astype(BF16)

    for p in range(PIECES):
        glow[:, p * 128 : p * 128 + 128] = greps[p].astype(BF16)

    hidden_t = hidden[...].T
    for j in range(4):
        rhs = jnp.concatenate(
            [glow[:, j * 128 : j * 128 + 128], glow[:, 512 + j * 128 : 512 + j * 128 + 128]], 1
        )
        sp_ref[:, :, j * 128 : j * 128 + 128] = stack_halves(mm(hidden_t, rhs))

    for j in range(3):
        cols = slice(j * 256, j * 256 + 256)
        ghid[:, cols] = mm_nt(glow[...], wpiece_ref[cols, :]).astype(BF16)

    ctx_t = ctx[...].T
    for j in range(3):
        rhs = jnp.concatenate(
            [ghid[:, j * 128 : j * 128 + 128], ghid[:, 384 + j * 128 : 384 + j * 128 + 128]], 1
        )
        so_ref[:, :, j * 128 : j * 128 + 128] = stack_halves(mm(ctx_t, rhs))

    for j in range(3):
        cols = slice(j * 256, j * 256 + 256)
        gctx[:, cols] = mm_nt(ghid[...], wout_ref[cols, :]).astype(BF16)

    @pl.loop(0, PAIRS)
    def _(p):
        q = qkv[p]
        k = qkv[PAIRS + p]
        v = qkv[2 * PAIRS + p]
        g = gctx[:, lanes(p)]
        dk = [None, None]
        dv = [None, None]
        for rb in range(2):
            rs = slice(rb * 256, rb * 256 + 256)
            n = (rb + 1) * 256
            dq = []
            for head in range(2):
                gh = head_part(g[rs], head)
                qh = head_part(q[rs], head)
                pr_low = prob[p, head, rs, :n]
                pr = pr_low.astype(F32)
                dp = mm_nt(gh, v[:n])
                inner = jnp.sum(dp * pr, -1, keepdims=True)
                ds = (pr * (dp - inner)).astype(BF16)
                dq.append(mm(ds, k[:n]))
                dv_now = mm_tn(pr_low, gh)
                dk_now = mm_tn(ds, qh)
                for half in range(rb + 1):
                    hs = slice(half * 256, half * 256 + 256)
                    dv[half] = dv_now[hs] if dv[half] is None else dv[half] + dv_now[hs]
                    dk[half] = dk_now[hs] if dk[half] is None else dk[half] + dk_now[hs]
            dqkv[rs, lanes(p)] = (jnp.where(low_lanes, dq[0], dq[1]) * 0.125).astype(BF16)
        for half in range(2):
            hs = slice(half * 256, half * 256 + 256)
            dqkv[hs, lanes(PAIRS + p)] = dk[half].astype(BF16)
            dqkv[hs, lanes(2 * PAIRS + p)] = dv[half].astype(BF16)

    normed_t[...] = normed[...].T

    @pl.loop(0, 9)
    def _(j):
        rhs = jnp.concatenate([dqkv[:, lanes(j)], dqkv[:, lanes(9 + j)]], 1)
        sq_ref[:, :, lanes(j)] = stack_halves(mm(normed_t[...], rhs))

    for j in range(3):
        cols = slice(j * 256, j * 256 + 256)
        gnorm[:, cols] = mm_nt(dqkv[...], wqkv_ref[cols, :])

    x = x_ref[:, :D].astype(F32)
    inv_rms = lax.rsqrt(jnp.mean(x * x, -1, keepdims=True) + EPSILON)
    x_hat = x * inv_rms
    gn = gnorm[...]
    ggain = jnp.sum(gn * x_hat, 0, keepdims=True)
    gh = gn * gain
    gx = inv_rms * (gh - x_hat * jnp.mean(gh * x_hat, -1, keepdims=True))
    gb = (gx + ghid[...].astype(F32)).astype(BF16)
    gb_ref[...] = gb.reshape(WIN, SLOT, D)

    feature = lax.broadcasted_iota(jnp.int32, (ROWS, D), 1)
    block = lax.broadcasted_iota(jnp.int32, (ROWS, D), 0) // SLOT
    spread = jnp.where(feature // 24 == block, ggain, 0.0).astype(BF16)
    pick = lax.broadcasted_iota(jnp.int32, (D, 128), 0) % 24
    pick = jnp.where(pick == lax.broadcasted_iota(jnp.int32, (D, 128), 1), 1.0, 0.0).astype(BF16)
    sg_ref[...] = mm(spread, pick).astype(BF16).reshape(WIN, SLOT, 128)


def owner_step(x, gain, w_qkv, w_out, w_piece, table):
    vmem = pl.BlockSpec(memory_space=pltpu.VMEM)
    return pl.pallas_call(
        owner_kernel,
        out_shape=(
            jax.ShapeDtypeStruct((WIN, SLOT, D), BF16),
            jax.ShapeDtypeStruct((WIN, 48, 1152), BF16),
            jax.ShapeDtypeStruct((WIN, 48, 384), BF16),
            jax.ShapeDtypeStruct((WIN, 48, 512), BF16),
            jax.ShapeDtypeStruct((CODES, R), BF16),
            jax.ShapeDtypeStruct((WIN, SLOT, 128), BF16),
        ),
        in_specs=[vmem] * 6,
        out_specs=(vmem,) * 6,
        scratch_shapes=[
            pltpu.VMEM((ROWS, D), BF16),
            pltpu.VMEM((D, ROWS), BF16),
            pltpu.VMEM((18, ROWS, 128), BF16),
            pltpu.VMEM((PAIRS, 2, ROWS, ROWS), BF16),
            pltpu.VMEM((ROWS, D), BF16),
            pltpu.VMEM((ROWS, D), BF16),
            pltpu.VMEM((PIECES, ROWS, R), BF16),
            pltpu.VMEM((PIECES, R, ROWS), BF16),
            pltpu.VMEM((PIECES, ROWS, R), F32),
            pltpu.VMEM((ROWS, PIECES * R), BF16),
            pltpu.VMEM((ROWS, D), BF16),
            pltpu.VMEM((ROWS, D), BF16),
            pltpu.VMEM((ROWS, 3 * D), BF16),
            pltpu.VMEM((ROWS, ROWS), F32),
            pltpu.VMEM((3, ROWS, 128), F32),
            pltpu.VMEM((R, CODES), F32),
            pltpu.VMEM((ROWS, D), F32),
        ],
        compiler_params=pltpu.CompilerParams(vmem_limit_bytes=56 * 1024 * 1024),
        cost_estimate=pl.CostEstimate(
            flops=26_000_000_000, bytes_accessed=16_000_000, transcendentals=20_000_000
        ),
        name="owner_step",
    )(x, gain, w_qkv, w_out, w_piece, table)


ITEMS = (
    ("t", 128, 128, "zx"),
    ("p", 48, 512, "xz"),
    ("o", 48, 384, "zx"),
    ("q0", 48, 640, "xz"),
    ("q1", 48, 512, "zx"),
    ("g", 16, 128, "xz"),
)
N_ITEMS = len(ITEMS)


def remote(src, dst, sems, index, where):
    return pltpu.make_async_remote_copy(
        src_ref=src,
        dst_ref=dst,
        send_sem=sems[0].at[index],
        recv_sem=sems[1].at[index],
        device_id=where,
        device_id_type=MESH,
    )


def reduce_kernel(
    gb_ref, sq_ref, so_ref, sp_ref, st_ref, sg_ref, hot_ref, rows_ref, gain_ref, qkv_ref, out_ref, piece_ref, tab_ref, *scratch
):
    landed, send_rows, recv_rows, send_sem, recv_sem = scratch[:5]
    bufs = [scratch[5 + 7 * i : 12 + 7 * i] for i in range(N_ITEMS)]
    sems = (send_sem, recv_sem)
    me = lax.axis_index("win")
    y = lax.axis_index("rep")
    core = lax.rem(me, 2)
    z = lax.rem(me // 2, 4)
    x = me // 8

    barrier = pltpu.get_barrier_semaphore()

    @pl.loop(1, WIN)
    def _(k):
        pl.semaphore_signal(
            barrier, inc=1, device_id={"win": lax.rem(me + k, WIN)}, device_id_type=MESH
        )

    @pl.loop(1, 4)
    def _(k):
        pl.semaphore_signal(
            barrier, inc=1, device_id={"rep": lax.rem(y + k, 4)}, device_id_type=MESH
        )

    pl.semaphore_wait(barrier, WIN - 1 + 3)

    sources = {
        "t": st_ref,
        "p": sp_ref,
        "o": so_ref,
        "q0": sq_ref.at[:, :, :, :, pl.ds(0, 640)],
        "q1": sq_ref.at[:, :, :, :, pl.ds(640, 512)],
        "g": sg_ref,
    }

    def at_xz(ref, order, first, second=None):
        if order == "xz":
            return ref.at[first] if second is None else ref.at[first, second]
        return ref.at[:, first] if second is None else ref.at[second, first]

    def win_of(order, step, k):
        if order[step] == "x":
            return lax.rem(x + k, 4) * 8 + z * 2 + core
        return x * 8 + lax.rem(z + k, 4) * 2 + core

    def place_of(order, step, k):
        return lax.rem((x if order[step] == "x" else z) + k, 4)

    def core_copy(i):
        name = ITEMS[i][0]
        return remote(
            sources[name].at[:, :, 1 - core], bufs[i][0], sems, (i, 0), {"win": me + 1 - 2 * core}
        )

    def ring_copy(i, step, k):
        order = ITEMS[i][3]
        if step == 0:
            src = at_xz(bufs[i][1], order, place_of(order, 0, k))
        else:
            src = bufs[i][3].at[place_of(order, 1, k)]
        return remote(
            src,
            bufs[i][2 + 2 * step].at[k - 1],
            sems,
            (i, 1 + 3 * step + k - 1),
            {"win": win_of(order, step, k)},
        )

    def last_copy(i, k):
        return remote(
            bufs[i][5].at[lax.rem(y + k, 4)],
            bufs[i][6].at[k - 1],
            sems,
            (i, 7 + k - 1),
            {"rep": lax.rem(y + k, 4)},
        )

    for i in range(N_ITEMS):
        core_copy(i).start()
    exchange_rows(gb_ref, landed, send_rows, recv_rows, me)
    landed[me] = gb_ref[me]

    for i in range(N_ITEMS):
        core_copy(i).wait()
        src, got, acc = sources[ITEMS[i][0]], bufs[i][0], bufs[i][1]
        for a in range(4):

            @pl.loop(0, 4)
            def _(b):
                acc[a, b] = (src[a, b, core].astype(F32) + got[a, b].astype(F32)).astype(BF16)

        for k in (2, 1, 3):
            ring_copy(i, 0, k).start()

    for i in range(N_ITEMS):
        order = ITEMS[i][3]
        for k in (2, 1, 3):
            ring_copy(i, 0, k).wait()
        got, acc = bufs[i][2], bufs[i][3]

        @pl.loop(0, 4)
        def _(b):
            total = at_xz(bufs[i][1], order, place_of(order, 0, 0), b)[...].astype(F32)
            for k in range(3):
                total += got[k, b].astype(F32)
            acc[b] = total.astype(BF16)

        for k in (2, 1, 3):
            ring_copy(i, 1, k).start()

    for i in range(N_ITEMS):
        name, rows, width, order = ITEMS[i]
        for k in (2, 1, 3):
            ring_copy(i, 1, k).wait()
        got = bufs[i][4]
        total = bufs[i][3][place_of(order, 1, 0)].astype(F32)
        for k in range(3):
            total += got[k].astype(F32)
        low = bufs[i][5]
        if name == "t":
            low[...] = total.astype(BF16).reshape(4, 32, 128)
        elif name == "g":
            for yy in range(4):
                low[yy] = total.astype(BF16)
        else:
            wide = scratch[-1]
            wide[:, 24:] = jnp.zeros((2, 8, 640), F32)
            for half in range(2):
                for t in range(3):
                    at = t * 16 + half * 8
                    wide[half, t * 8 : t * 8 + 8, :width] = total[at : at + 8]
            for yy in range(4):
                both = jnp.concatenate(
                    [wide[0, 6 * yy : 6 * yy + 8, :width], wide[1, 6 * yy : 6 * yy + 8, :width]], 0
                )
                low[yy] = both.astype(BF16)
        for k in (2, 1, 3):
            last_copy(i, k).start()

    factor = 1.0 / math.sqrt(EVENTS * WIN * 4)
    for i in range(N_ITEMS):
        name, rows, width, order = ITEMS[i]
        for k in (2, 1, 3):
            last_copy(i, k).wait()
        got = bufs[i][6]
        total = bufs[i][5][y].astype(F32)
        for k in range(3):
            total += got[k].astype(F32)
        total = total * factor
        if name == "t":
            tab_ref[...] = total
        elif name == "g":
            gain_ref[...] = total[:8]
        else:
            dst, base, half = {
                "p": (piece_ref, 0, 512),
                "o": (out_ref, 0, 384),
                "q0": (qkv_ref, 0, 1152),
                "q1": (qkv_ref, 640, 1152),
            }[name]
            dst[:, base : base + width] = total[:6]
            dst[:, half + base : half + base + width] = total[8:14]

    wait_rows(gb_ref, landed, send_rows, recv_rows, me)
    rows_ref[...] = mm_tn(hot_ref[...], landed[...].reshape(ROWS, D)).astype(BF16)


def reduce_all(gb, sq, so, sp, st, sg, hot):
    vmem = pl.BlockSpec(memory_space=pltpu.VMEM)
    scratch = [
        pltpu.VMEM((WIN, SLOT, D), BF16),
        pltpu.SemaphoreType.DMA((WIN,)),
        pltpu.SemaphoreType.DMA((WIN,)),
        pltpu.SemaphoreType.DMA((N_ITEMS, 10)),
        pltpu.SemaphoreType.DMA((N_ITEMS, 10)),
    ]
    for name, rows, width, order in ITEMS:
        last = {"t": 32, "g": 16}.get(name, 16)
        scratch += [
            pltpu.VMEM((4, 4, rows, width), BF16),
            pltpu.VMEM((4, 4, rows, width), BF16),
            pltpu.VMEM((3, 4, rows, width), BF16),
            pltpu.VMEM((4, rows, width), BF16),
            pltpu.VMEM((3, rows, width), BF16),
            pltpu.VMEM((4, last, width), BF16),
            pltpu.VMEM((3, last, width), BF16),
        ]
    scratch.append(pltpu.VMEM((2, 32, 640), F32))
    return pl.pallas_call(
        reduce_kernel,
        out_shape=(
            jax.ShapeDtypeStruct((EVENTS, D), BF16),
            jax.ShapeDtypeStruct((8, 128), F32),
            jax.ShapeDtypeStruct((6, 3 * D), F32),
            jax.ShapeDtypeStruct((6, D), F32),
            jax.ShapeDtypeStruct((6, PIECES * R), F32),
            jax.ShapeDtypeStruct((32, R), F32),
        ),
        in_specs=[vmem] * 7,
        out_specs=(vmem,) * 6,
        scratch_shapes=scratch,
        compiler_params=pltpu.CompilerParams(
            collective_id=2, has_side_effects=True, vmem_limit_bytes=56 * 1024 * 1024
        ),
        name="reduce_all",
    )(
        gb,
        sq.reshape(4, 4, 2, 48, 1152),
        so.reshape(4, 4, 2, 48, 384),
        sp.reshape(4, 4, 2, 48, 512),
        st.reshape(4, 4, 2, 128, 128),
        sg.reshape(4, 4, 2, 16, 128),
        hot,
    )


def body(
    events,
    send_counts,
    patient_ids,
    codes,
    event_piece,
    censor_piece,
    norm_gain,
    w_qkv,
    w_out,
    w_piece,
    code_table,
):
    labels = jnp.concatenate([patient_ids[0], codes[0], event_piece[0], censor_piece[0]], 0)
    received, hot = dispatch(events[0, 0], labels, send_counts[0])
    gb, sq, so, sp, st, sg = owner_step(
        received.reshape(ROWS, WIDE), norm_gain[None], w_qkv, w_out, w_piece, code_table
    )
    rows, gain, g_qkv, g_out, g_piece, g_table = reduce_all(gb, sq, so, sp, st, sg, hot)
    y = lax.axis_index("rep")
    g_gain = lax.dynamic_slice(gain[0], (6 * y,), (6,))
    return (rows[None, None], g_gain, g_qkv, g_out, g_piece, g_table)


def solution(mesh):
    split = P("win", "rep")
    return jax.shard_map(
        body,
        mesh=mesh,
        in_specs=(split,) * 6 + (P(),) * 5,
        out_specs=(split,) + (P(("win", "rep")),) * 5,
        check_vma=False,
    )
```

time: 1320 us -> 179 us (0.14); the launches traced: 1300 us -> 178 us
  blocking collectives: 431 us -> 0 us
  starting transfers between devices: 294 us -> 0 us
  matrix products: 275 us -> 0 us
  local copies, waits for them, and re-layouts: 217 us -> 13.1 us
  Pallas kernels: 0 us -> 164 us
  other arithmetic: 62.7 us -> 0.74 us
  between operations: 15.3 us -> 0.67 us
    unnamed x2 -> x0, blocking collectives: 431 us -> none
    dot_general x117 -> x0, matrix products: 275 us -> none  [the longest x8 68.8 us: one_piece(): jnp.dot(reps_now, code_table.T, preferred_element_type=jnp.float32)]
    unnamed x96 -> x0, starting transfers between devices: 267 us -> none
    pallas_call x0 -> x3, Pallas kernels: none -> 164 us  [the longest x1 88 us: owner_step(): pl.pallas_call(owner_kernel, out_shape=(jax.ShapeDtypeStruct((WIN, SLOT,...]
    unnamed x108 -> x13, local copies, waits for them, and re-layouts: 164 us -> 10.6 us
    all_to_all x4 -> x0, starting transfers between devices: 27.3 us -> none  [the longest x1 8.38 us: body(): lax.all_to_all(counts_out[:, None], 'win', split_axis=0, concat_axis=0, t...]
    gather x7 -> x0, local copies, waits for them, and re-layouts: 23.5 us -> none  [the longest x1 4.55 us: uncompact(): grad_block[take_index]]
  transfers between devices with their start and end apart: 101 -> 0, of which waited for: 3 -> 0; matrix products, arithmetic and copies ran while one was open for 45% -> 0% of each run, Pallas kernels for 0% -> 0%
where the time goes in v1:
time: 179 us; the launch traced here: 178 us
  Pallas kernels  164 us (92%)
  local copies, waits for them, and re-layouts  13.1 us (7%)
    pallas_call x1, Pallas kernels, owner_step(): pl.pallas_call(owner_kernel, out_shape=(jax.ShapeDtypeStruct((WIN, SLOT,...  88 us
    pallas_call x1, Pallas kernels, reduce_all(): pl.pallas_call(reduce_kernel, out_shape=(jax.ShapeDtypeStruct((EVENTS, D)...  56.6 us
    pallas_call x1, Pallas kernels, dispatch(): pl.pallas_call(dispatch_kernel, out_shape=(jax.ShapeDtypeStruct((WIN, SLO...  19.1 us
    unnamed x13, local copies, waits for them, and re-layouts  10.6 us

profile of v1, /device:TPU:0, one launch (start us, length us, event | category | flops | bytes accessed | tf_op | source)
XLA Modules:
  0.0 178.2 jit_solution(17025896285906796533)
XLA Ops:
  0.6 0.7 pad_add_fusion.lab_ref
  1.4 0.0 copy-start
  1.4 1.0 copy-done
  2.4 0.0 copy-start.2
  2.4 0.7 copy-done.2
  3.0 19.1 %dispatch.1 = (bf16[32,16,896]{2,1,0:T(8,128)(2,1)S(1)}, bf16[512,256]{1,0:T(8,128)(2,1)S(1)}) custom-call(bf16[256,768]{1,0:T(8,128)(2,1)S(1)} %bitcast.15, s32[4,256]{1,0:T(4,128)S(1)} %pad_add_fusion.lab_ref, s32[1,32]{1,0:T(1,128)S(1)} %bitcast.16), custom_call_target="tpu_custom_call" | custom-call | tf_op jit(solution)/shard_map/dispatch/pallas_call | solution.py:115
  22.1 0.0 copy-start.1
  22.1 0.7 copy-done.1
  22.8 0.0 copy-start.3
  22.8 0.9 copy-done.3
  23.8 1.3 broadcast_in_dim.6.gain_ref
  25.0 88.0 %owner_step.1 = (bf16[32,16,768]{2,1,0:T(8,128)(2,1)}, bf16[32,48,1152]{2,1,0:T(8,128)(2,1)}, bf16[32,48,384]{2,1,0:T(8,128)(2,1)}, bf16[32,48,512]{2,1,0:T(8,12...) custom-call(bf16[512,896]{1,0:T(8,128)(2,1)} %bitcast.17, f32[1,768]{1,0:T(1,128)} %broadcast_in_dim.6.gain_ref, ...), custom_call_target="tpu_custom_call" | custom-call | flops 25999998976 | bytes 16000000 | tf_op jit(solution)/shard_map/owner_step/pallas_call | solution.py:363
  113.0 56.6 %reduce_all.1 = (bf16[256,768]{1,0:T(8,128)(2,1)}, f32[8,128]{1,0:T(8,128)}, f32[6,2304]{1,0:T(8,128)}, f32[6,768]{1,0:T(8,128)}, f32[6,1024]{1,0:T(8,128)}, /*index=5*/f32[32,128]{1,0:T(8,128)}) custom-call(bf16[32,16,768]{2,1,0:T(8,128)(2,1)} %get-tuple-element.21.gb_ref, bf16[4,4,2,48,1152]{4,3,2,1,0:T(8,128)(2,1)} %bitcast.18, ...), custom_call_target="tpu_custom_call" | custom-call | tf_op jit(solution)/shard_map/reduce_all/pallas_call | solution.py:614
  169.6 0.7 slice.3
  170.3 0.6 dynamic-slice_bitcast_fusion
  170.9 1.8 copy.22
  172.6 1.5 copy.23
  174.2 1.3 copy.24
  175.5 1.4 copy.25
  176.9 1.3 copy.26
Async XLA Ops:
  1.4 1.0 copy-start
  2.4 0.7 copy-start.2
  22.1 0.7 copy-start.1
  22.8 0.9 copy-start.3

commit v2 on v1

v2 whole, which is shorter than its diff:
```python
import functools
import math

import jax
import jax.numpy as jnp
from jax import lax
from jax.experimental import pallas as pl
from jax.experimental.pallas import tpu as pltpu
from jax.sharding import PartitionSpec as P

HEADS = 12
EPSILON = 1e-05
MESH = pl.DeviceIdType.MESH

D = 768
PAIRS = 6
PIECES = 8
CODES = 4096
R = 128
ROWS = 512
EVENTS = 256
WIN = 32
SLOT = 16
LAB = 128
WIDE = D + LAB
BLOCK = 2048

F32 = jnp.float32
BF16 = jnp.bfloat16

NT = (((1,), (1,)), ((), ()))
TN = (((0,), (0,)), ((), ()))


def mm(a, b):
    return jnp.dot(a, b, preferred_element_type=F32)


def mm_nt(a, b):
    return lax.dot_general(a, b, NT, preferred_element_type=F32)


def mm_tn(a, b):
    return lax.dot_general(a, b, TN, preferred_element_type=F32)


def exchange_rows(src_ref, dst_ref, send_sem, recv_sem, me):
    @pl.loop(1, WIN)
    def _(k):
        peer = lax.rem(me + k, WIN)
        pltpu.make_async_remote_copy(
            src_ref=src_ref.at[peer],
            dst_ref=dst_ref.at[me],
            send_sem=send_sem.at[k],
            recv_sem=recv_sem.at[k],
            device_id={"win": peer},
            device_id_type=MESH,
        ).start()


def wait_rows(src_ref, dst_ref, send_sem, recv_sem, me):
    @pl.loop(1, WIN)
    def _(k):
        sender = lax.rem(me + WIN - k, WIN)
        pltpu.make_async_remote_copy(
            src_ref=src_ref.at[me],
            dst_ref=dst_ref.at[sender],
            send_sem=send_sem.at[k],
            recv_sem=recv_sem.at[k],
            device_id={"win": sender},
            device_id_type=MESH,
        ).wait()


def stack_halves(res):
    tiles = res.reshape(WIN, 3, 8, 256)
    both = jnp.concatenate([tiles[..., :128], tiles[..., 128:]], 2)
    return both.reshape(WIN, 48, 128).astype(BF16)


def lanes(index):
    return pl.ds(pl.multiple_of(index * 128, 128), 128)


ITEMS = (
    ("t", 128, 128, "zx"),
    ("p", 48, 512, "xz"),
    ("o", 48, 384, "zx"),
    ("a0", 48, 256, "xz"),
    ("b0", 48, 128, "zx"),
    ("a1", 48, 256, "zx"),
    ("b1", 48, 128, "xz"),
    ("a2", 48, 256, "xz"),
    ("b2", 48, 128, "zx"),
    ("g", 16, 128, "zx"),
)
N_ITEMS = len(ITEMS)
INDEX = {item[0]: i for i, item in enumerate(ITEMS)}


def remote(src, dst, sems, index, where):
    return pltpu.make_async_remote_copy(
        src_ref=src,
        dst_ref=dst,
        send_sem=sems[0].at[index],
        recv_sem=sems[1].at[index],
        device_id=where,
        device_id_type=MESH,
    )


def step_kernel(
    ev_ref,
    lab_ref,
    cnt_ref,
    gain_ref,
    wqkv_any,
    wout_any,
    wpiece_any,
    table_any,
    rows_ref,
    gain_out,
    qkv_ref,
    out_ref,
    piece_ref,
    tab_ref,
    wqkv,
    wout,
    wpiece,
    table_ref,
    load_sem,
    hot_ref,
    packed,
    landed,
    rows_out,
    returned,
    there_send,
    there_recv,
    back_send,
    back_recv,
    sum_send,
    sum_recv,
    src_t,
    src_p,
    src_o,
    src_a,
    src_b,
    src_g,
    tiles,
    normed,
    normed_t,
    qkv,
    prob,
    ctx,
    hidden,
    reps,
    reps_t,
    greps,
    glow,
    ghid,
    gctx,
    dqkv,
    bias,
    labs,
    gtab_t,
    gnorm,
    *spare,
):
    bufs = [spare[6 * i : 6 * i + 6] for i in range(N_ITEMS)]
    sems = (sum_send, sum_recv)
    me = lax.axis_index("win")
    y = lax.axis_index("rep")
    core = lax.rem(me, 2)
    z_at = lax.rem(me // 2, 4)
    x_at = me // 8

    barrier = pltpu.get_barrier_semaphore()

    @pl.loop(1, WIN)
    def _(k):
        pl.semaphore_signal(
            barrier, inc=1, device_id={"win": lax.rem(me + k, WIN)}, device_id_type=MESH
        )

    @pl.loop(1, 4)
    def _(k):
        pl.semaphore_signal(
            barrier, inc=1, device_id={"rep": lax.rem(y + k, 4)}, device_id_type=MESH
        )

    loads = [
        pltpu.make_async_copy(src, dst, load_sem.at[i])
        for i, (src, dst) in enumerate(
            ((wqkv_any, wqkv), (wout_any, wout), (wpiece_any, wpiece), (table_any, table_ref))
        )
    ]
    for load in loads:
        load.start()

    counts = cnt_ref[...].astype(F32)
    row = lax.broadcasted_iota(jnp.int32, (ROWS, WIN), 0)
    owner = lax.broadcasted_iota(jnp.int32, (ROWS, WIN), 1)
    row_owner = row // SLOT
    mine = jnp.sum(jnp.where(owner == row_owner, counts, 0.0), 1, keepdims=True)
    start = jnp.sum(jnp.where(owner < row_owner, counts, 0.0), 1, keepdims=True)
    offset = (lax.broadcasted_iota(jnp.int32, (ROWS, 1), 0) % SLOT).astype(F32)
    place = lax.broadcasted_iota(jnp.int32, (ROWS, EVENTS), 1).astype(F32)
    wanted = jnp.where(offset < mine, start + offset, -1.0)
    hot = jnp.where(place == wanted, 1.0, 0.0).astype(BF16)
    hot_ref[...] = hot
    packed[:, :, :D] = mm(hot, ev_ref[...]).astype(BF16).reshape(WIN, SLOT, D)

    lab = lab_ref[...]
    high = lab[1:2] // 64
    rows = [lab[0:1], high, lab[1:2] - high * 64, lab[2:3], jnp.maximum(lab[2:3], lab[3:4])]
    rows.append(jnp.ones((1, EVENTS), jnp.int32))
    rows.append(jnp.zeros((2, EVENTS), jnp.int32))
    table = jnp.concatenate(rows, 0).astype(F32)
    table = jnp.concatenate([table, jnp.zeros((LAB - 8, EVENTS), F32)], 0).astype(BF16)
    packed[:, :, D:] = mm_nt(hot, table).astype(BF16).reshape(WIN, SLOT, LAB)

    pl.semaphore_wait(barrier, WIN - 1 + 3)
    exchange_rows(packed, landed, there_send, there_recv, me)
    landed[me] = packed[me]
    wait_rows(packed, landed, there_send, there_recv, me)

    sources = {"t": src_t, "p": src_p, "o": src_o, "g": src_g}
    for s in range(3):
        sources["a%d" % s] = src_a.at[s]
        sources["b%d" % s] = src_b.at[s]

    def place_of(order, step, k):
        return lax.rem((x_at if order[step] == "x" else z_at) + k, 4)

    def win_of(order, step, k):
        if order[step] == "x":
            return lax.rem(x_at + k, 4) * 8 + z_at * 2 + core
        return x_at * 8 + lax.rem(z_at + k, 4) * 2 + core

    def blocked(name):
        _, rows, width, _ = ITEMS[INDEX[name]]
        return sources[name].reshape(4, 4, 2, rows, width)

    def buf(name):
        return bufs[INDEX[name]]

    def core_copy(name):
        i = INDEX[name]
        return remote(
            blocked(name).at[:, :, 1 - core], buf(name)[0], sems, (i, 0), {"win": me + 1 - 2 * core}
        )

    def at_xz(ref, order, first, second=None):
        if order == "xz":
            return ref.at[first] if second is None else ref.at[first, second]
        return ref.at[:, first] if second is None else ref.at[second, first]

    def ring_copy(name, step, k):
        i = INDEX[name]
        order = ITEMS[i][3]
        if step == 0:
            src = at_xz(buf(name)[0], order, place_of(order, 0, k))
        else:
            src = buf(name)[2].at[place_of(order, 1, k)]
        return remote(
            src,
            buf(name)[1 + 2 * step].at[k - 1],
            sems,
            (i, 1 + 3 * step + k - 1),
            {"win": win_of(order, step, k)},
        )

    def last_copy(name, k):
        return remote(
            buf(name)[4].at[lax.rem(y + k, 4)],
            buf(name)[5].at[k - 1],
            sems,
            (INDEX[name], 7 + k - 1),
            {"rep": lax.rem(y + k, 4)},
        )

    def begin(name):
        core_copy(name).start()

    def to_first_ring(name):
        core_copy(name).wait()
        src, got = blocked(name), buf(name)[0]
        for a in range(4):

            @pl.loop(0, 4)
            def _(b):
                got[a, b] = (src[a, b, core].astype(F32) + got[a, b].astype(F32)).astype(BF16)

        for k in (2, 1, 3):
            ring_copy(name, 0, k).start()

    def to_second_ring(name):
        order = ITEMS[INDEX[name]][3]
        for k in (2, 1, 3):
            ring_copy(name, 0, k).wait()
        mine, got, acc = buf(name)[0], buf(name)[1], buf(name)[2]

        @pl.loop(0, 4)
        def _(b):
            total = at_xz(mine, order, place_of(order, 0, 0), b)[...].astype(F32)
            for k in range(3):
                total += got[k, b].astype(F32)
            acc[b] = total.astype(BF16)

        for k in (2, 1, 3):
            ring_copy(name, 1, k).start()

    def to_last(name):
        _, rows, width, order = ITEMS[INDEX[name]]
        for k in (2, 1, 3):
            ring_copy(name, 1, k).wait()
        got = buf(name)[3]
        total = buf(name)[2][place_of(order, 1, 0)].astype(F32)
        for k in range(3):
            total += got[k].astype(F32)
        low = buf(name)[4]
        if name == "t":
            low[...] = total.astype(BF16).reshape(4, 32, 128)
        elif name == "g":
            for yy in range(4):
                low[yy] = (pltpu.roll(total, 128 - 6 * yy, 1) if yy else total).astype(BF16)
        else:
            for half in range(2):
                for t in range(3):
                    at = t * 16 + half * 8
                    tiles[half, t * 8 : t * 8 + 8, :width] = total[at : at + 8]
            for yy in range(4):
                both = jnp.concatenate(
                    [tiles[0, 6 * yy : 6 * yy + 8, :width], tiles[1, 6 * yy : 6 * yy + 8, :width]], 0
                )
                low[yy] = both.astype(BF16)
        for k in (2, 1, 3):
            last_copy(name, k).start()

    def finish(name):
        _, rows, width, order = ITEMS[INDEX[name]]
        for k in (2, 1, 3):
            last_copy(name, k).wait()
        got = buf(name)[5]
        total = buf(name)[4][y].astype(F32)
        for k in range(3):
            total += got[k].astype(F32)
        total = total * (1.0 / math.sqrt(EVENTS * WIN * 4))
        if name == "t":
            tab_ref[...] = total
        elif name == "g":
            gain_out[...] = total[:8]
        else:
            for u in range(width // 128):
                if name == "p":
                    dst, at = piece_ref, u * 256
                elif name == "o":
                    dst, at = out_ref, u * 256
                else:
                    part = u if name[0] == "a" else 2
                    dst, at = qkv_ref, part * D + int(name[1]) * 256
                us = slice(u * 128, u * 128 + 128)
                dst[:, at : at + 128] = total[:6, us]
                dst[:, at + 128 : at + 256] = total[8:14, us]

    gain = gain_ref[...]
    lab = landed[:, :, D:].reshape(ROWS, LAB).astype(F32)
    valid = lab[:, 5:6] > 0.5
    patient = jnp.where(valid, lab[:, 0:1], -1.0)
    labs[0] = jnp.broadcast_to(lab[:, 1:2] * 64.0 + lab[:, 2:3], (ROWS, 128))
    labs[1] = jnp.broadcast_to(jnp.where(valid, lab[:, 3:4], -1.0), (ROWS, 128))
    labs[2] = jnp.broadcast_to(jnp.where(valid, lab[:, 4:5], -1.0), (ROWS, 128))

    lab_t = lab.T
    patient_row = jnp.where(lab_t[5:6] > 0.5, lab_t[0:1], -1.0)
    row = lax.broadcasted_iota(jnp.int32, (ROWS, ROWS), 0)
    col = lax.broadcasted_iota(jnp.int32, (ROWS, ROWS), 1)
    allowed = ((patient == patient_row) & (col <= row)) | (col == row)
    bias[...] = jnp.where(allowed, 0.0, -1e30)

    x = landed[:, :, :D].reshape(ROWS, D).astype(F32)
    inv_rms = lax.rsqrt(jnp.mean(x * x, -1, keepdims=True) + EPSILON)
    normed[...] = (x * inv_rms * gain).astype(BF16)

    loads[0].wait()

    @pl.loop(0, 9)
    def _(j):
        cols = pl.ds(pl.multiple_of(j * 256, 256), 256)
        res = mm(normed[...], wqkv[:, cols])
        scale = jnp.where(j < 3, 0.125, 1.0)
        res = (res * scale).astype(BF16)
        qkv[2 * j] = res[:, :128]
        qkv[2 * j + 1] = res[:, 128:]

    low_lanes = lax.broadcasted_iota(jnp.int32, (1, 128), 1) < 64

    def head_part(value, head):
        zero = jnp.zeros((), value.dtype)
        return jnp.where(low_lanes, value, zero) if head == 0 else jnp.where(low_lanes, zero, value)

    @pl.loop(0, PAIRS)
    def _(p):
        q = qkv[p]
        k = qkv[PAIRS + p]
        v = qkv[2 * PAIRS + p]
        for rb in range(2):
            rs = slice(rb * 256, rb * 256 + 256)
            n = (rb + 1) * 256
            parts = []
            for head in range(2):
                s = mm_nt(head_part(q[rs], head), k[:n]) + bias[rs, :n]
                w = jnp.exp(s - jnp.max(s, -1, keepdims=True))
                pr = (w * (1.0 / jnp.sum(w, -1, keepdims=True))).astype(BF16)
                prob[p, head, rs, :n] = pr
                parts.append(mm(pr, v[:n]))
            ctx[rs, lanes(p)] = jnp.where(low_lanes, parts[0], parts[1]).astype(BF16)

    loads[1].wait()

    @pl.loop(0, 3)
    def _(j):
        cols = pl.ds(pl.multiple_of(j * 256, 256), 256)
        res = mm(ctx[...], wout[:, cols])
        hidden[:, cols] = (landed[:, :, cols].reshape(ROWS, 256).astype(F32) + res).astype(BF16)

    loads[2].wait()

    @pl.loop(0, 4)
    def _(j):
        cols = pl.ds(pl.multiple_of(j * 256, 256), 256)
        res = mm(hidden[...], wpiece[:, cols])
        for i in range(2):
            part = res[:, i * 128 : i * 128 + 128]
            reps[2 * j + i] = part.astype(BF16)
            reps_t[2 * j + i] = part.T.astype(BF16)

    loads[3].wait()
    log_codes = math.log(CODES)
    times = BLOCK // 128

    def widen(tile):
        return jnp.concatenate([tile] * times, 1)

    greps[...] = jnp.zeros_like(greps)

    @pl.loop(0, CODES // BLOCK)
    def _(b):
        codes_at = pl.ds(pl.multiple_of(b * BLOCK, BLOCK), BLOCK)
        tab = table_ref[codes_at, :]
        ids = (b * BLOCK + lax.broadcasted_iota(jnp.int32, (1, BLOCK), 1)).astype(F32)
        gtab_t[:, codes_at] = jnp.zeros((R, BLOCK), F32)

        @pl.loop(0, PIECES)
        def _(p):
            piece = p.astype(F32)
            code, event, end = labs[0], labs[1], labs[2]
            at_row = jnp.where(end >= piece, -log_codes, -1e30)
            at_code = jnp.where(event >= piece, -log_codes, -1e30)
            target = jnp.where(event == piece, 1.0, 0.0)
            logits = mm_nt(reps[p], tab)
            is_code = widen(code) == ids
            e = jnp.exp(logits + jnp.where(is_code, widen(at_code), widen(at_row)))
            g = (e - jnp.where(is_code, widen(target), 0.0)).astype(BF16)
            greps[p] += mm(g, tab)
            gtab_t[:, codes_at] += mm(reps_t[p], g)

        blocks = BLOCK // 128
        turned = gtab_t[:, codes_at].T.astype(BF16).reshape(blocks, 128, 128)
        src_t[pl.ds(b * blocks, blocks)] = turned

    begin("t")

    for p in range(PIECES):
        glow[:, p * 128 : p * 128 + 128] = greps[p].astype(BF16)

    hidden_t = hidden[...].T
    for j in range(4):
        cols = slice(j * 256, j * 256 + 256)
        src_p[:, :, j * 128 : j * 128 + 128] = stack_halves(mm(hidden_t, glow[:, cols]))
    begin("p")

    for j in range(3):
        cols = slice(j * 256, j * 256 + 256)
        ghid[:, cols] = mm_nt(glow[...], wpiece[cols, :]).astype(BF16)

    ctx_t = ctx[...].T
    for j in range(3):
        cols = slice(j * 256, j * 256 + 256)
        src_o[:, :, j * 128 : j * 128 + 128] = stack_halves(mm(ctx_t, ghid[:, cols]))
    begin("o")

    for j in range(3):
        cols = slice(j * 256, j * 256 + 256)
        gctx[:, cols] = mm_nt(ghid[...], wout[cols, :]).astype(BF16)
    normed_t[...] = normed[...].T
    to_first_ring("t")

    def backward_pair(p):
        q = qkv[p]
        k = qkv[PAIRS + p]
        v = qkv[2 * PAIRS + p]
        g = gctx[:, lanes(p)]
        dk = [None, None]
        dv = [None, None]
        for rb in range(2):
            rs = slice(rb * 256, rb * 256 + 256)
            n = (rb + 1) * 256
            dq = []
            for head in range(2):
                gh = head_part(g[rs], head)
                qh = head_part(q[rs], head)
                pr_low = prob[p, head, rs, :n]
                pr = pr_low.astype(F32)
                dp = mm_nt(gh, v[:n])
                inner = jnp.sum(dp * pr, -1, keepdims=True)
                ds = (pr * (dp - inner)).astype(BF16)
                dq.append(mm(ds, k[:n]))
                dv_now = mm_tn(pr_low, gh)
                dk_now = mm_tn(ds, qh)
                for half in range(rb + 1):
                    hs = slice(half * 256, half * 256 + 256)
                    dv[half] = dv_now[hs] if dv[half] is None else dv[half] + dv_now[hs]
                    dk[half] = dk_now[hs] if dk[half] is None else dk[half] + dk_now[hs]
            dqkv[rs, lanes(p)] = (jnp.where(low_lanes, dq[0], dq[1]) * 0.125).astype(BF16)
        for half in range(2):
            hs = slice(half * 256, half * 256 + 256)
            dqkv[hs, lanes(PAIRS + p)] = dk[half].astype(BF16)
            dqkv[hs, lanes(2 * PAIRS + p)] = dv[half].astype(BF16)

    def backward_step(s):
        pl.loop(2 * s, 2 * s + 2)(backward_pair)

    def qkv_step(s):
        for part in range(3):
            cols = slice(part * D + s * 256, part * D + s * 256 + 256)
            res = stack_halves(mm(normed_t[...], dqkv[:, cols]))
            if part < 2:
                src_a[s, :, :, part * 128 : part * 128 + 128] = res
            else:
                src_b[s] = res
        begin("a%d" % s)
        begin("b%d" % s)

    backward_step(0)
    to_first_ring("p")
    to_first_ring("o")
    qkv_step(0)
    to_second_ring("t")
    backward_step(1)
    to_first_ring("a0")
    to_first_ring("b0")
    qkv_step(1)
    to_second_ring("p")
    to_second_ring("o")
    to_last("t")
    backward_step(2)
    to_first_ring("a1")
    to_first_ring("b1")
    qkv_step(2)
    to_second_ring("a0")
    to_second_ring("b0")

    for j in range(3):
        cols = slice(j * 256, j * 256 + 256)
        gnorm[:, cols] = mm_nt(dqkv[...], wqkv[cols, :])

    x = landed[:, :, :D].reshape(ROWS, D).astype(F32)
    inv_rms = lax.rsqrt(jnp.mean(x * x, -1, keepdims=True) + EPSILON)
    x_hat = x * inv_rms
    gn = gnorm[...]
    ggain = jnp.sum(gn * x_hat, 0, keepdims=True)
    gh = gn * gain
    gx = inv_rms * (gh - x_hat * jnp.mean(gh * x_hat, -1, keepdims=True))
    gb = (gx + ghid[...].astype(F32)).astype(BF16)
    rows_out[...] = gb.reshape(WIN, SLOT, D)

    exchange_rows(rows_out, returned, back_send, back_recv, me)
    returned[me] = rows_out[me]

    feature = lax.broadcasted_iota(jnp.int32, (ROWS, D), 1)
    block = lax.broadcasted_iota(jnp.int32, (ROWS, D), 0) // SLOT
    spread = jnp.where(feature // 24 == block, ggain, 0.0).astype(BF16)
    pick = lax.broadcasted_iota(jnp.int32, (D, 128), 0) % 24
    pick = jnp.where(pick == lax.broadcasted_iota(jnp.int32, (D, 128), 1), 1.0, 0.0).astype(BF16)
    src_g[...] = mm(spread, pick).astype(BF16).reshape(WIN, SLOT, 128)
    begin("g")
    to_first_ring("a2")
    to_first_ring("b2")
    to_second_ring("a1")
    to_second_ring("b1")
    to_last("p")
    to_last("o")
    to_first_ring("g")
    to_last("a0")
    to_last("b0")
    to_second_ring("a2")
    to_second_ring("b2")
    to_last("a1")
    to_last("b1")
    to_second_ring("g")
    to_last("a2")
    to_last("b2")
    to_last("g")
    for name in ("t", "p", "o", "a0", "b0", "a1", "b1"):
        finish(name)
    wait_rows(rows_out, returned, back_send, back_recv, me)
    rows_ref[...] = mm_tn(hot_ref[...], returned[...].reshape(ROWS, D)).astype(BF16)
    for name in ("a2", "b2", "g"):
        finish(name)


def step(events, labels, counts, gain, w_qkv, w_out, w_piece, table):
    vmem = pl.BlockSpec(memory_space=pltpu.VMEM)
    scratch = [
        pltpu.VMEM((D, 3 * D), BF16),
        pltpu.VMEM((D, D), BF16),
        pltpu.VMEM((D, PIECES * R), BF16),
        pltpu.VMEM((CODES, R), BF16),
        pltpu.SemaphoreType.DMA((4,)),
        pltpu.VMEM((ROWS, EVENTS), BF16),
        pltpu.VMEM((WIN, SLOT, WIDE), BF16),
        pltpu.VMEM((WIN, SLOT, WIDE), BF16),
        pltpu.VMEM((WIN, SLOT, D), BF16),
        pltpu.VMEM((WIN, SLOT, D), BF16),
        pltpu.SemaphoreType.DMA((WIN,)),
        pltpu.SemaphoreType.DMA((WIN,)),
        pltpu.SemaphoreType.DMA((WIN,)),
        pltpu.SemaphoreType.DMA((WIN,)),
        pltpu.SemaphoreType.DMA((N_ITEMS, 10)),
        pltpu.SemaphoreType.DMA((N_ITEMS, 10)),
        pltpu.VMEM((WIN, 128, 128), BF16),
        pltpu.VMEM((WIN, 48, 512), BF16),
        pltpu.VMEM((WIN, 48, 384), BF16),
        pltpu.VMEM((3, WIN, 48, 256), BF16),
        pltpu.VMEM((3, WIN, 48, 128), BF16),
        pltpu.VMEM((WIN, SLOT, 128), BF16),
        pltpu.VMEM((2, 32, 512), F32),
        pltpu.VMEM((ROWS, D), BF16),
        pltpu.VMEM((D, ROWS), BF16),
        pltpu.VMEM((18, ROWS, 128), BF16),
        pltpu.VMEM((PAIRS, 2, ROWS, ROWS), BF16),
        pltpu.VMEM((ROWS, D), BF16),
        pltpu.VMEM((ROWS, D), BF16),
        pltpu.VMEM((PIECES, ROWS, R), BF16),
        pltpu.VMEM((PIECES, R, ROWS), BF16),
        pltpu.VMEM((PIECES, ROWS, R), F32),
        pltpu.VMEM((ROWS, PIECES * R), BF16),
        pltpu.VMEM((ROWS, D), BF16),
        pltpu.VMEM((ROWS, D), BF16),
        pltpu.VMEM((ROWS, 3 * D), BF16),
        pltpu.VMEM((ROWS, ROWS), F32),
        pltpu.VMEM((3, ROWS, 128), F32),
        pltpu.VMEM((R, CODES), F32),
        pltpu.VMEM((ROWS, D), F32),
    ]
    for name, rows, width, order in ITEMS:
        last = 32 if name == "t" else 16
        scratch += [
            pltpu.VMEM((4, 4, rows, width), BF16),
            pltpu.VMEM((3, 4, rows, width), BF16),
            pltpu.VMEM((4, rows, width), BF16),
            pltpu.VMEM((3, rows, width), BF16),
            pltpu.VMEM((4, last, width), BF16),
            pltpu.VMEM((3, last, width), BF16),
        ]
    return pl.pallas_call(
        step_kernel,
        out_shape=(
            jax.ShapeDtypeStruct((EVENTS, D), BF16),
            jax.ShapeDtypeStruct((8, 128), F32),
            jax.ShapeDtypeStruct((6, 3 * D), F32),
            jax.ShapeDtypeStruct((6, D), F32),
            jax.ShapeDtypeStruct((6, PIECES * R), F32),
            jax.ShapeDtypeStruct((32, R), F32),
        ),
        in_specs=[vmem] * 4 + [pl.BlockSpec(memory_space=pl.ANY)] * 4,
        out_specs=(vmem,) * 6,
        scratch_shapes=scratch,
        compiler_params=pltpu.CompilerParams(
            collective_id=1, has_side_effects=True, vmem_limit_bytes=62 * 1024 * 1024
        ),
        name="step",
    )(events, labels, counts, gain, w_qkv, w_out, w_piece, table)


def result_kernel(*refs):
    for src, dst in zip(refs[:5], refs[6:11]):
        dst[...] = src[...]
    refs[11][...] = refs[5][0, :6]


def results(rows, g_qkv, g_out, g_piece, g_table, gain):
    vmem = pl.BlockSpec(memory_space=pltpu.VMEM)
    like = [jax.ShapeDtypeStruct(a.shape, a.dtype) for a in (rows, g_qkv, g_out, g_piece, g_table)]
    return pl.pallas_call(
        result_kernel,
        out_shape=(*like, jax.ShapeDtypeStruct((6,), F32)),
        in_specs=[vmem] * 6,
        out_specs=(vmem,) * 6,
        name="results",
    )(rows, g_qkv, g_out, g_piece, g_table, gain)


def body(
    events,
    send_counts,
    patient_ids,
    codes,
    event_piece,
    censor_piece,
    norm_gain,
    w_qkv,
    w_out,
    w_piece,
    code_table,
):
    labels = jnp.concatenate([patient_ids[0], codes[0], event_piece[0], censor_piece[0]], 0)
    rows, gain, g_qkv, g_out, g_piece, g_table = step(
        events[0, 0], labels, send_counts[0], norm_gain[None], w_qkv, w_out, w_piece, code_table
    )
    rows, g_qkv, g_out, g_piece, g_table, g_gain = results(rows, g_qkv, g_out, g_piece, g_table, gain)
    return (rows[None, None], g_gain, g_qkv, g_out, g_piece, g_table)


def solution(mesh):
    split = P("win", "rep")
    return jax.shard_map(
        body,
        mesh=mesh,
        in_specs=(split,) * 6 + (P(),) * 5,
        out_specs=(split,) + (P(("win", "rep")),) * 5,
        check_vma=False,
    )
```

time: 179 us -> 136 us (0.76)
  Pallas kernels: 164 us -> 133 us
  local copies, waits for them, and re-layouts: 13.1 us -> 1.27 us
    pallas_call x3 -> x2, Pallas kernels: 164 us -> 133 us  [the longest x1 131 us: step(): pl.pallas_call(step_kernel, out_shape=(jax.ShapeDtypeStruct((EVENTS, D),...]
    unnamed x13 -> x0, local copies, waits for them, and re-layouts: 10.6 us -> none
where the time goes in v2:
time: 136 us
  Pallas kernels  133 us (98%)
    pallas_call x1, Pallas kernels, step(): pl.pallas_call(step_kernel, out_shape=(jax.ShapeDtypeStruct((EVENTS, D),...  131 us

profile of v2, /device:TPU:0, one launch (start us, length us, event | category | flops | bytes accessed | tf_op | source)
XLA Modules:
  0.0 135.8 jit_solution(10836659231879891044)
XLA Ops:
  0.6 1.3 broadcast_in_dim.6.gain_ref
  1.9 1.3 pad_add_fusion.lab_ref
  3.2 130.7 %step.1 = (bf16[256,768]{1,0:T(8,128)(2,1)}, f32[8,128]{1,0:T(8,128)}, f32[6,2304]{1,0:T(8,128)}, f32[6,768]{1,0:T(8,128)}, f32[6,1024]{1,0:T(8,128)}, /*index=5*/f32[32,128]{1,0:T(8,128)}) custom-call(bf16[256,768]{1,0:T(8,128)(2,1)} %bitcast.7, s32[4,256]{1,0:T(4,128)} %pad_add_fusion.lab_ref, s32[1,32]{1,0:T(1,128)} %bitcast.12, ...), custom_call_target="tpu_custom_call" | custom-call | tf_op jit(solution)/shard_map/step/pallas_call | solution.py:667
  133.9 1.9 %results.1 = (bf16[256,768]{1,0:T(8,128)(2,1)}, f32[6,2304]{1,0:T(8,128)}, f32[6,768]{1,0:T(8,128)}, f32[6,1024]{1,0:T(8,128)}, f32[32,128]{1,0:T(8,128)}, /*index=5*/f32[6]{0:T(128)}) custom-call(bf16[256,768]{1,0:T(8,128)(2,1)} %get-tuple-element.18.refs_0_, f32[6,2304]{1,0:T(8,128)} %get-tuple-element.19.refs_1_, f32[6,768]{1,0:T(8,128)} %get-tuple-element.20.refs_2_, ...), custom_call_target="tpu_custom_call" | custom-call | tf_op jit(solution)/shard_map/results/pallas_call | solution.py:696

commit v3 on v2

--- a/solution.py
+++ b/solution.py
@@ -23,7 +23,8 @@
 SLOT = 16
 LAB = 128
 WIDE = D + LAB
-BLOCK = 2048
+BLOCK = 1024
+LOG2E = math.log2(math.e)
 
 F32 = jnp.float32
 BF16 = jnp.bfloat16
@@ -76,6 +77,17 @@
     tiles = res.reshape(WIN, 3, 8, 256)
     both = jnp.concatenate([tiles[..., :128], tiles[..., 128:]], 2)
     return both.reshape(WIN, 48, 128).astype(BF16)
+
+
+TODO = [(rb, head) for rb in range(2) for head in range(2)]
+
+
+def span(rb):
+    return slice(rb * 256, rb * 256 + 256)
+
+
+def far(rb):
+    return rb * 256 + 256
 
 
 def lanes(index):
@@ -156,13 +168,14 @@
     reps,
     reps_t,
     greps,
+    own_row,
+    fix,
     glow,
     ghid,
     gctx,
     dqkv,
     bias,
     labs,
-    gtab_t,
     gnorm,
     *spare,
 ):
@@ -399,22 +412,21 @@
         zero = jnp.zeros((), value.dtype)
         return jnp.where(low_lanes, value, zero) if head == 0 else jnp.where(low_lanes, zero, value)
 
-    @pl.loop(0, PAIRS)
+    @pl.loop(0, PAIRS, unroll=2)
     def _(p):
         q = qkv[p]
         k = qkv[PAIRS + p]
         v = qkv[2 * PAIRS + p]
+        s = [mm_nt(head_part(q[span(rb)], head), k[: far(rb)]) + bias[span(rb), : far(rb)] for rb, head in TODO]
+        top = [jnp.max(a, -1, keepdims=True) for a in s]
+        w = [jnp.exp(a - m) for a, m in zip(s, top)]
+        inv = [1.0 / jnp.sum(a, -1, keepdims=True) for a in w]
+        pr = [(a * i).astype(BF16) for a, i in zip(w, inv)]
+        for (rb, head), a in zip(TODO, pr):
+            prob[p, head, span(rb), : far(rb)] = a
+        got = [mm(a, v[: far(rb)]) for (rb, head), a in zip(TODO, pr)]
         for rb in range(2):
-            rs = slice(rb * 256, rb * 256 + 256)
-            n = (rb + 1) * 256
-            parts = []
-            for head in range(2):
-                s = mm_nt(head_part(q[rs], head), k[:n]) + bias[rs, :n]
-                w = jnp.exp(s - jnp.max(s, -1, keepdims=True))
-                pr = (w * (1.0 / jnp.sum(w, -1, keepdims=True))).astype(BF16)
-                prob[p, head, rs, :n] = pr
-                parts.append(mm(pr, v[:n]))
-            ctx[rs, lanes(p)] = jnp.where(low_lanes, parts[0], parts[1]).astype(BF16)
+            ctx[span(rb), lanes(p)] = jnp.where(low_lanes, got[2 * rb], got[2 * rb + 1]).astype(BF16)
 
     loads[1].wait()
 
@@ -436,38 +448,56 @@
             reps_t[2 * j + i] = part.T.astype(BF16)
 
     loads[3].wait()
-    log_codes = math.log(CODES)
+
+    log_codes = math.log2(CODES)
     times = BLOCK // 128
+    code, event, end = labs[0], labs[1], labs[2]
+    own_code = jnp.where(event >= 0, code, -1.0)
 
     def widen(tile):
         return jnp.concatenate([tile] * times, 1)
 
-    greps[...] = jnp.zeros_like(greps)
+    def block_ids(b):
+        return (b * BLOCK + lax.broadcasted_iota(jnp.int32, (1, BLOCK), 1)).astype(F32)
+
+    def block_at(b):
+        return pl.ds(pl.multiple_of(b * BLOCK, BLOCK), BLOCK)
+
+    own_row[...] = jnp.zeros_like(own_row)
 
     @pl.loop(0, CODES // BLOCK)
     def _(b):
-        codes_at = pl.ds(pl.multiple_of(b * BLOCK, BLOCK), BLOCK)
-        tab = table_ref[codes_at, :]
-        ids = (b * BLOCK + lax.broadcasted_iota(jnp.int32, (1, BLOCK), 1)).astype(F32)
-        gtab_t[:, codes_at] = jnp.zeros((R, BLOCK), F32)
-
-        @pl.loop(0, PIECES)
-        def _(p):
-            piece = p.astype(F32)
-            code, event, end = labs[0], labs[1], labs[2]
-            at_row = jnp.where(end >= piece, -log_codes, -1e30)
-            at_code = jnp.where(event >= piece, -log_codes, -1e30)
-            target = jnp.where(event == piece, 1.0, 0.0)
-            logits = mm_nt(reps[p], tab)
-            is_code = widen(code) == ids
-            e = jnp.exp(logits + jnp.where(is_code, widen(at_code), widen(at_row)))
-            g = (e - jnp.where(is_code, widen(target), 0.0)).astype(BF16)
+        hot = jnp.where(widen(own_code) == block_ids(b), 1.0, 0.0).astype(BF16)
+        own_row[...] += mm(hot, table_ref[block_at(b), :])
+
+    for p in range(PIECES):
+        at_code = jnp.sum(reps[p].astype(F32) * own_row[...], -1, keepdims=True)
+        value = jnp.exp2(at_code * LOG2E - log_codes) - 1.0
+        fix[p] = jnp.where(event == p, value, 0.0)
+
+    greps[...] = jnp.zeros_like(greps)
+
+    @pl.loop(0, CODES // BLOCK)
+    def _(b):
+        tab = table_ref[block_at(b), :]
+        ids = block_ids(b)
+
+        def weights(p, logits):
+            live = widen(jnp.where(end >= p, -log_codes, -1e30))
+            e = jnp.exp2(logits * LOG2E + live)
+            act = widen(jnp.where(event <= p, own_code, -1.0))
+            return jnp.where(act == ids, widen(fix[p]), e).astype(BF16)
+
+        logits = mm_nt(reps[0], tab)
+        total = jnp.zeros((R, BLOCK), F32)
+        for p in range(PIECES):
+            after = mm_nt(reps[p + 1], tab) if p + 1 < PIECES else None
+            g = weights(p, logits)
             greps[p] += mm(g, tab)
-            gtab_t[:, codes_at] += mm(reps_t[p], g)
-
-        blocks = BLOCK // 128
-        turned = gtab_t[:, codes_at].T.astype(BF16).reshape(blocks, 128, 128)
-        src_t[pl.ds(b * blocks, blocks)] = turned
+            total = total + mm(reps_t[p], g)
+            logits = after
+        turned = total.T.astype(BF16).reshape(BLOCK // 128, 128, 128)
+        src_t[pl.ds(b * (BLOCK // 128), BLOCK // 128)] = turned
 
     begin("t")
 
@@ -501,35 +531,26 @@
         k = qkv[PAIRS + p]
         v = qkv[2 * PAIRS + p]
         g = gctx[:, lanes(p)]
-        dk = [None, None]
-        dv = [None, None]
+        gh = [head_part(g[span(rb)], head) for rb, head in TODO]
+        low = [prob[p, head, span(rb), : far(rb)] for rb, head in TODO]
+        dp = [mm_nt(a, v[: far(rb)]) for (rb, head), a in zip(TODO, gh)]
+        inner = [jnp.sum(a * b.astype(F32), -1, keepdims=True) for a, b in zip(dp, low)]
+        ds = [(b.astype(F32) * (a - i)).astype(BF16) for a, b, i in zip(dp, low, inner)]
+        cat = lambda a, i: jnp.concatenate([a[i], a[i + 1]], 0)
+        dv = [mm_tn(cat(low, i), cat(gh, i)) for i in (0, 2)]
+        dq = [mm(a, k[: far(rb)]) for (rb, head), a in zip(TODO, ds)]
+        qh = [head_part(q[span(rb)], head) for rb, head in TODO]
+        dk = [mm_tn(cat(ds, i), cat(qh, i)) for i in (0, 2)]
         for rb in range(2):
-            rs = slice(rb * 256, rb * 256 + 256)
-            n = (rb + 1) * 256
-            dq = []
-            for head in range(2):
-                gh = head_part(g[rs], head)
-                qh = head_part(q[rs], head)
-                pr_low = prob[p, head, rs, :n]
-                pr = pr_low.astype(F32)
-                dp = mm_nt(gh, v[:n])
-                inner = jnp.sum(dp * pr, -1, keepdims=True)
-                ds = (pr * (dp - inner)).astype(BF16)
-                dq.append(mm(ds, k[:n]))
-                dv_now = mm_tn(pr_low, gh)
-                dk_now = mm_tn(ds, qh)
-                for half in range(rb + 1):
-                    hs = slice(half * 256, half * 256 + 256)
-                    dv[half] = dv_now[hs] if dv[half] is None else dv[half] + dv_now[hs]
-                    dk[half] = dk_now[hs] if dk[half] is None else dk[half] + dk_now[hs]
-            dqkv[rs, lanes(p)] = (jnp.where(low_lanes, dq[0], dq[1]) * 0.125).astype(BF16)
-        for half in range(2):
-            hs = slice(half * 256, half * 256 + 256)
-            dqkv[hs, lanes(PAIRS + p)] = dk[half].astype(BF16)
-            dqkv[hs, lanes(2 * PAIRS + p)] = dv[half].astype(BF16)
+            both = jnp.where(low_lanes, dq[2 * rb], dq[2 * rb + 1]) * 0.125
+            dqkv[span(rb), lanes(p)] = both.astype(BF16)
+        for at, parts in ((PAIRS, dk), (2 * PAIRS, dv)):
+            wide = parts[1]
+            dqkv[:256, lanes(at + p)] = (wide[:256] + parts[0]).astype(BF16)
+            dqkv[256:, lanes(at + p)] = wide[256:].astype(BF16)
 
     def backward_step(s):
-        pl.loop(2 * s, 2 * s + 2)(backward_pair)
+        pl.loop(2 * s, 2 * s + 2, unroll=2)(backward_pair)
 
     def qkv_step(s):
         for part in range(3):
@@ -645,13 +666,14 @@
         pltpu.VMEM((PIECES, ROWS, R), BF16),
         pltpu.VMEM((PIECES, R, ROWS), BF16),
         pltpu.VMEM((PIECES, ROWS, R), F32),
+        pltpu.VMEM((ROWS, R), F32),
+        pltpu.VMEM((PIECES, ROWS, 128), F32),
         pltpu.VMEM((ROWS, PIECES * R), BF16),
         pltpu.VMEM((ROWS, D), BF16),
         pltpu.VMEM((ROWS, D), BF16),
         pltpu.VMEM((ROWS, 3 * D), BF16),
         pltpu.VMEM((ROWS, ROWS), F32),
         pltpu.VMEM((3, ROWS, 128), F32),
-        pltpu.VMEM((R, CODES), F32),
         pltpu.VMEM((ROWS, D), F32),
     ]
     for name, rows, width, order in ITEMS:
@@ -678,7 +700,7 @@
         out_specs=(vmem,) * 6,
         scratch_shapes=scratch,
         compiler_params=pltpu.CompilerParams(
-            collective_id=1, has_side_effects=True, vmem_limit_bytes=62 * 1024 * 1024
+            collective_id=1, has_side_effects=True, vmem_limit_bytes=63 * 1024 * 1024
         ),
         name="step",
     )(events, labels, counts, gain, w_qkv, w_out, w_piece, table)

time: 136 us -> 122 us (0.90)
  Pallas kernels: 133 us -> 119 us
    pallas_call x1, Pallas kernels: 131 us -> 117 us  [step(): pl.pallas_call(step_kernel, out_shape=(jax.ShapeDtypeStruct((EVENTS, D),...]
where the time goes in v3:
time: 122 us
  Pallas kernels  119 us (98%)
  other arithmetic  1.33 us (1%)
  local copies, waits for them, and re-layouts  1.27 us (1%)
    pallas_call x1, Pallas kernels, step(): pl.pallas_call(step_kernel, out_shape=(jax.ShapeDtypeStruct((EVENTS, D),...  117 us

profile of v3, /device:TPU:0, one launch (start us, length us, event | category | flops | bytes accessed | tf_op | source)
XLA Modules:
  0.0 122.2 jit_solution(15782084707490549487)
XLA Ops:
  0.6 1.3 %broadcast_in_dim.6.gain_ref = f32[1,768]{1,0:T(1,128)} reshape(f32[768]{0:T(1024)} %param.17) | data formatting | bytes 6144 | tf_op jit(solution)/shard_map/broadcast_in_dim | solution.py:742
  1.9 1.3 %pad_add_fusion.lab_ref = s32[4,256]{1,0:T(4,128)} fusion(s32[1,256]{1,0:T(1,128)} %bitcast.8, s32[1,256]{1,0:T(1,128)} %bitcast.9, s32[1,256]{1,0:T(1,128)} %bitcast.10, s32[1,256]{1,0:T(1,128)} %bitcast.11), kind=kLoop, calls=%fused_computation | loop fusion | flops 3072 | bytes 8192 | tf_op jit(solution)/shard_map/concatenate | solution.py:740
  3.2 117.1 %step.1 = (bf16[256,768]{1,0:T(8,128)(2,1)}, f32[8,128]{1,0:T(8,128)}, f32[6,2304]{1,0:T(8,128)}, f32[6,768]{1,0:T(8,128)}, f32[6,1024]{1,0:T(8,128)}, /*index=5*/f32[32,128]{1,0:T(8,128)}) custom-call(bf16[256,768]{1,0:T(8,128)(2,1)} %bitcast.7, s32[4,256]{1,0:T(4,128)} %pad_add_fusion.lab_ref, s32[1,32]{1,0:T(1,128)} %bitcast.12, ...), custom_call_target="tpu_custom_call" | custom-call | tf_op jit(solution)/shard_map/step/pallas_call | solution.py:689
  120.4 1.9 %results.1 = (bf16[256,768]{1,0:T(8,128)(2,1)}, f32[6,2304]{1,0:T(8,128)}, f32[6,768]{1,0:T(8,128)}, f32[6,1024]{1,0:T(8,128)}, f32[32,128]{1,0:T(8,128)}, /*index=5*/f32[6]{0:T(128)}) custom-call(bf16[256,768]{1,0:T(8,128)(2,1)} %get-tuple-element.18.refs_0_, f32[6,2304]{1,0:T(8,128)} %get-tuple-element.19.refs_1_, f32[6,768]{1,0:T(8,128)} %get-tuple-element.20.refs_2_, ...), custom_call_target="tpu_custom_call" | custom-call | tf_op jit(solution)/shard_map/results/pallas_call | solution.py:718

commit v4 on v3

--- a/solution.py
+++ b/solution.py
@@ -45,8 +45,8 @@
     return lax.dot_general(a, b, TN, preferred_element_type=F32)
 
 
-def exchange_rows(src_ref, dst_ref, send_sem, recv_sem, me):
-    @pl.loop(1, WIN)
+def exchange_rows(src_ref, dst_ref, send_sem, recv_sem, me, low=1, high=WIN):
+    @pl.loop(low, high)
     def _(k):
         peer = lax.rem(me + k, WIN)
         pltpu.make_async_remote_copy(
@@ -95,16 +95,20 @@
 
 
 ITEMS = (
-    ("t", 128, 128, "zx"),
-    ("p", 48, 512, "xz"),
-    ("o", 48, 384, "zx"),
-    ("a0", 48, 256, "xz"),
-    ("b0", 48, 128, "zx"),
-    ("a1", 48, 256, "zx"),
-    ("b1", 48, 128, "xz"),
-    ("a2", 48, 256, "xz"),
-    ("b2", 48, 128, "zx"),
-    ("g", 16, 128, "zx"),
+    ("t", 128, 128, "zxy"),
+    ("p", 48, 512, "yxz"),
+    ("oa", 48, 256, "zxy"),
+    ("ob", 48, 128, "xzy"),
+    ("q0", 48, 128, "xzy"),
+    ("k0", 48, 128, "zxy"),
+    ("v0", 48, 128, "yxz"),
+    ("q1", 48, 128, "xzy"),
+    ("k1", 48, 128, "zxy"),
+    ("v1", 48, 128, "yxz"),
+    ("q2", 48, 128, "xzy"),
+    ("k2", 48, 128, "zxy"),
+    ("v2", 48, 128, "yxz"),
+    ("g", 16, 128, "zxy"),
 )
 N_ITEMS = len(ITEMS)
 INDEX = {item[0]: i for i, item in enumerate(ITEMS)}
@@ -152,12 +156,16 @@
     back_recv,
     sum_send,
     sum_recv,
+    tab_send,
+    tab_recv,
     src_t,
     src_p,
-    src_o,
-    src_a,
-    src_b,
+    src_oa,
+    src_ob,
+    src_qkv,
     src_g,
+    perm,
+    turned_p,
     tiles,
     normed,
     normed_t,
@@ -235,20 +243,32 @@
     pl.semaphore_wait(barrier, WIN - 1 + 3)
     exchange_rows(packed, landed, there_send, there_recv, me)
     landed[me] = packed[me]
+
+    at = lax.broadcasted_iota(jnp.int32, (D, 1), 0)
+    group, inner = at // 24, at % 24
+    z_of, r_of = inner // 6, inner % 6
+    y_of, x_of, core_of = group // 8, (group // 2) % 4, group % 2
+    feature = ((x_of * 4 + z_of) * 2 + core_of) * 24 + y_of * 6 + r_of
+    chosen = lax.broadcasted_iota(jnp.int32, (D, D), 1) == feature
+    perm[...] = jnp.where(chosen, 1.0, 0.0).astype(BF16)
+
     wait_rows(packed, landed, there_send, there_recv, me)
 
-    sources = {"t": src_t, "p": src_p, "o": src_o, "g": src_g}
+    sources = {"t": src_t, "p": src_p, "oa": src_oa, "ob": src_ob, "g": src_g}
     for s in range(3):
-        sources["a%d" % s] = src_a.at[s]
-        sources["b%d" % s] = src_b.at[s]
-
-    def place_of(order, step, k):
-        return lax.rem((x_at if order[step] == "x" else z_at) + k, 4)
-
-    def win_of(order, step, k):
-        if order[step] == "x":
-            return lax.rem(x_at + k, 4) * 8 + z_at * 2 + core
-        return x_at * 8 + lax.rem(z_at + k, 4) * 2 + core
+        for part in range(3):
+            sources["qkv"[part] + str(s)] = src_qkv.at[s, part]
+    mine_at = {"x": x_at, "y": y, "z": z_at}
+
+    def place_of(axis, k):
+        return lax.rem(mine_at[axis] + k, 4)
+
+    def device_of(axis, k):
+        if axis == "x":
+            return {"win": place_of("x", k) * 8 + z_at * 2 + core}
+        if axis == "z":
+            return {"win": x_at * 8 + place_of("z", k) * 2 + core}
+        return {"rep": place_of("y", k)}
 
     def blocked(name):
         _, rows, width, _ = ITEMS[INDEX[name]]
@@ -263,8 +283,8 @@
             blocked(name).at[:, :, 1 - core], buf(name)[0], sems, (i, 0), {"win": me + 1 - 2 * core}
         )
 
-    def at_xz(ref, order, first, second=None):
-        if order == "xz":
+    def block_of(ref, order, first, second=None):
+        if order in ("xzy", "yxz"):
             return ref.at[first] if second is None else ref.at[first, second]
         return ref.at[:, first] if second is None else ref.at[second, first]
 
@@ -272,25 +292,52 @@
         i = INDEX[name]
         order = ITEMS[i][3]
         if step == 0:
-            src = at_xz(buf(name)[0], order, place_of(order, 0, k))
+            src = block_of(buf(name)[0], order, place_of(order[0], k))
         else:
-            src = buf(name)[2].at[place_of(order, 1, k)]
+            src = buf(name)[2].at[place_of(order[1], k)]
         return remote(
             src,
             buf(name)[1 + 2 * step].at[k - 1],
             sems,
             (i, 1 + 3 * step + k - 1),
-            {"win": win_of(order, step, k)},
+            device_of(order[step], k),
         )
 
     def last_copy(name, k):
+        axis = ITEMS[INDEX[name]][3][2]
         return remote(
-            buf(name)[4].at[lax.rem(y + k, 4)],
+            buf(name)[4].at[place_of(axis, k)],
             buf(name)[5].at[k - 1],
             sems,
             (INDEX[name], 7 + k - 1),
-            {"rep": lax.rem(y + k, 4)},
+            device_of(axis, k),
         )
+
+    def table_core(b):
+        return remote(
+            blocked("t").at[b, :, 1 - core],
+            buf("t")[0].at[b],
+            (tab_send, tab_recv),
+            (b, 0),
+            {"win": me + 1 - 2 * core},
+        )
+
+    def table_ring(b, k):
+        return remote(
+            buf("t")[0].at[b, place_of("z", k)],
+            buf("t")[1].at[k - 1, b],
+            (tab_send, tab_recv),
+            (b, k),
+            device_of("z", k),
+        )
+
+    def table_to_ring(b):
+        table_core(b).wait()
+        src, got = blocked("t"), buf("t")[0]
+        for c in range(4):
+            got[b, c] = (src[b, c, core].astype(F32) + got[b, c].astype(F32)).astype(BF16)
+        for k in (2, 1, 3):
+            table_ring(b, k).start()
 
     def begin(name):
         core_copy(name).start()
@@ -309,13 +356,20 @@
 
     def to_second_ring(name):
         order = ITEMS[INDEX[name]][3]
-        for k in (2, 1, 3):
-            ring_copy(name, 0, k).wait()
+        if name == "t":
+
+            @pl.loop(0, 4)
+            def _(b):
+                for k in (2, 1, 3):
+                    table_ring(b, k).wait()
+        else:
+            for k in (2, 1, 3):
+                ring_copy(name, 0, k).wait()
         mine, got, acc = buf(name)[0], buf(name)[1], buf(name)[2]
 
         @pl.loop(0, 4)
         def _(b):
-            total = at_xz(mine, order, place_of(order, 0, 0), b)[...].astype(F32)
+            total = block_of(mine, order, place_of(order[0], 0), b)[...].astype(F32)
             for k in range(3):
                 total += got[k, b].astype(F32)
             acc[b] = total.astype(BF16)
@@ -328,7 +382,7 @@
         for k in (2, 1, 3):
             ring_copy(name, 1, k).wait()
         got = buf(name)[3]
-        total = buf(name)[2][place_of(order, 1, 0)].astype(F32)
+        total = buf(name)[2][place_of(order[1], 0)].astype(F32)
         for k in range(3):
             total += got[k].astype(F32)
         low = buf(name)[4]
@@ -355,7 +409,7 @@
         for k in (2, 1, 3):
             last_copy(name, k).wait()
         got = buf(name)[5]
-        total = buf(name)[4][y].astype(F32)
+        total = buf(name)[4][place_of(order[2], 0)].astype(F32)
         for k in range(3):
             total += got[k].astype(F32)
         total = total * (1.0 / math.sqrt(EVENTS * WIN * 4))
@@ -367,11 +421,10 @@
             for u in range(width // 128):
                 if name == "p":
                     dst, at = piece_ref, u * 256
-                elif name == "o":
-                    dst, at = out_ref, u * 256
+                elif name[0] == "o":
+                    dst, at = out_ref, u * 256 if name == "oa" else 512
                 else:
-                    part = u if name[0] == "a" else 2
-                    dst, at = qkv_ref, part * D + int(name[1]) * 256
+                    dst, at = qkv_ref, "qkv".index(name[0]) * D + int(name[1]) * 256
                 us = slice(u * 128, u * 128 + 128)
                 dst[:, at : at + 128] = total[:6, us]
                 dst[:, at + 128 : at + 256] = total[8:14, us]
@@ -498,16 +551,21 @@
             logits = after
         turned = total.T.astype(BF16).reshape(BLOCK // 128, 128, 128)
         src_t[pl.ds(b * (BLOCK // 128), BLOCK // 128)] = turned
-
-    begin("t")
+        table_core(b).start()
+
+        @pl.when(b > 0)
+        def _():
+            table_to_ring(b - 1)
+
+    table_to_ring(3)
 
     for p in range(PIECES):
         glow[:, p * 128 : p * 128 + 128] = greps[p].astype(BF16)
 
-    hidden_t = hidden[...].T
+    turned_p[...] = mm_nt(perm[...], hidden[...]).astype(BF16)
     for j in range(4):
         cols = slice(j * 256, j * 256 + 256)
-        src_p[:, :, j * 128 : j * 128 + 128] = stack_halves(mm(hidden_t, glow[:, cols]))
+        src_p[:, :, j * 128 : j * 128 + 128] = stack_halves(mm(turned_p[...], glow[:, cols]))
     begin("p")
 
     for j in range(3):
@@ -517,14 +575,23 @@
     ctx_t = ctx[...].T
     for j in range(3):
         cols = slice(j * 256, j * 256 + 256)
-        src_o[:, :, j * 128 : j * 128 + 128] = stack_halves(mm(ctx_t, ghid[:, cols]))
-    begin("o")
+        res = stack_halves(mm(ctx_t, ghid[:, cols]))
+        if j < 2:
+            src_oa[:, :, j * 128 : j * 128 + 128] = res
+        else:
+            src_ob[...] = res
+    begin("oa")
+    begin("ob")
+    to_first_ring("p")
 
     for j in range(3):
         cols = slice(j * 256, j * 256 + 256)
         gctx[:, cols] = mm_nt(ghid[...], wout[cols, :]).astype(BF16)
+    to_first_ring("oa")
+    to_first_ring("ob")
     normed_t[...] = normed[...].T
-    to_first_ring("t")
+    turned_p[...] = mm_nt(perm[...], normed[...]).astype(BF16)
+    to_second_ring("t")
 
     def backward_pair(p):
         q = qkv[p]
@@ -553,34 +620,28 @@
         pl.loop(2 * s, 2 * s + 2, unroll=2)(backward_pair)
 
     def qkv_step(s):
-        for part in range(3):
+        for part in (2, 0, 1):
             cols = slice(part * D + s * 256, part * D + s * 256 + 256)
-            res = stack_halves(mm(normed_t[...], dqkv[:, cols]))
-            if part < 2:
-                src_a[s, :, :, part * 128 : part * 128 + 128] = res
-            else:
-                src_b[s] = res
-        begin("a%d" % s)
-        begin("b%d" % s)
+            left = turned_p if part == 2 else normed_t
+            src_qkv[s, part] = stack_halves(mm(left[...], dqkv[:, cols]))
+            begin("qkv"[part] + str(s))
+
+    def each(stage, s):
+        for part in "vqk":
+            stage(part + str(s))
 
     backward_step(0)
-    to_first_ring("p")
-    to_first_ring("o")
     qkv_step(0)
-    to_second_ring("t")
+    to_last("t")
     backward_step(1)
-    to_first_ring("a0")
-    to_first_ring("b0")
+    each(to_first_ring, 0)
     qkv_step(1)
+    backward_step(2)
+    each(to_first_ring, 1)
+    qkv_step(2)
     to_second_ring("p")
-    to_second_ring("o")
-    to_last("t")
-    backward_step(2)
-    to_first_ring("a1")
-    to_first_ring("b1")
-    qkv_step(2)
-    to_second_ring("a0")
-    to_second_ring("b0")
+    to_second_ring("oa")
+    to_second_ring("ob")
 
     for j in range(3):
         cols = slice(j * 256, j * 256 + 256)
@@ -591,14 +652,6 @@
     x_hat = x * inv_rms
     gn = gnorm[...]
     ggain = jnp.sum(gn * x_hat, 0, keepdims=True)
-    gh = gn * gain
-    gx = inv_rms * (gh - x_hat * jnp.mean(gh * x_hat, -1, keepdims=True))
-    gb = (gx + ghid[...].astype(F32)).astype(BF16)
-    rows_out[...] = gb.reshape(WIN, SLOT, D)
-
-    exchange_rows(rows_out, returned, back_send, back_recv, me)
-    returned[me] = rows_out[me]
-
     feature = lax.broadcasted_iota(jnp.int32, (ROWS, D), 1)
     block = lax.broadcasted_iota(jnp.int32, (ROWS, D), 0) // SLOT
     spread = jnp.where(feature // 24 == block, ggain, 0.0).astype(BF16)
@@ -606,29 +659,36 @@
     pick = jnp.where(pick == lax.broadcasted_iota(jnp.int32, (D, 128), 1), 1.0, 0.0).astype(BF16)
     src_g[...] = mm(spread, pick).astype(BF16).reshape(WIN, SLOT, 128)
     begin("g")
-    to_first_ring("a2")
-    to_first_ring("b2")
-    to_second_ring("a1")
-    to_second_ring("b1")
+    each(to_first_ring, 2)
+
+    gh = gn * gain
+    gx = inv_rms * (gh - x_hat * jnp.mean(gh * x_hat, -1, keepdims=True))
+    gb = (gx + ghid[...].astype(F32)).astype(BF16)
+    rows_out[...] = gb.reshape(WIN, SLOT, D)
+    to_first_ring("g")
+    exchange_rows(rows_out, returned, back_send, back_recv, me, 1, 12)
+    each(to_second_ring, 0)
+    exchange_rows(rows_out, returned, back_send, back_recv, me, 12, 22)
     to_last("p")
-    to_last("o")
-    to_first_ring("g")
-    to_last("a0")
-    to_last("b0")
-    to_second_ring("a2")
-    to_second_ring("b2")
-    to_last("a1")
-    to_last("b1")
+    to_last("oa")
+    to_last("ob")
+    each(to_second_ring, 1)
+    exchange_rows(rows_out, returned, back_send, back_recv, me, 22, WIN)
+    returned[me] = rows_out[me]
     to_second_ring("g")
-    to_last("a2")
-    to_last("b2")
+    each(to_last, 0)
+    each(to_second_ring, 2)
+    each(to_last, 1)
     to_last("g")
-    for name in ("t", "p", "o", "a0", "b0", "a1", "b1"):
+    for name in ("t", "p", "oa", "ob"):
         finish(name)
+    each(finish, 0)
+    each(to_last, 2)
+    each(finish, 1)
     wait_rows(rows_out, returned, back_send, back_recv, me)
     rows_ref[...] = mm_tn(hot_ref[...], returned[...].reshape(ROWS, D)).astype(BF16)
-    for name in ("a2", "b2", "g"):
-        finish(name)
+    finish("g")
+    each(finish, 2)
 
 
 def step(events, labels, counts, gain, w_qkv, w_out, w_piece, table):
@@ -650,12 +710,16 @@
         pltpu.SemaphoreType.DMA((WIN,)),
         pltpu.SemaphoreType.DMA((N_ITEMS, 10)),
         pltpu.SemaphoreType.DMA((N_ITEMS, 10)),
+        pltpu.SemaphoreType.DMA((4, 4)),
+        pltpu.SemaphoreType.DMA((4, 4)),
         pltpu.VMEM((WIN, 128, 128), BF16),
         pltpu.VMEM((WIN, 48, 512), BF16),
-        pltpu.VMEM((WIN, 48, 384), BF16),
-        pltpu.VMEM((3, WIN, 48, 256), BF16),
-        pltpu.VMEM((3, WIN, 48, 128), BF16),
+        pltpu.VMEM((WIN, 48, 256), BF16),
+        pltpu.VMEM((WIN, 48, 128), BF16),
+        pltpu.VMEM((3, 3, WIN, 48, 128), BF16),
         pltpu.VMEM((WIN, SLOT, 128), BF16),
+        pltpu.VMEM((D, D), BF16),
+        pltpu.VMEM((D, ROWS), BF16),
         pltpu.VMEM((2, 32, 512), F32),
         pltpu.VMEM((ROWS, D), BF16),
         pltpu.VMEM((D, ROWS), BF16),

time: 122 us -> 119 us (0.975)
  Pallas kernels: 119 us -> 116 us
    pallas_call x1, Pallas kernels: 117 us -> 114 us  [step(): pl.pallas_call(step_kernel, out_shape=(jax.ShapeDtypeStruct((EVENTS, D),...]
where the time goes in v4:
time: 119 us
  Pallas kernels  116 us (97%)
  other arithmetic  1.33 us (1%)
  local copies, waits for them, and re-layouts  1.27 us (1%)
    pallas_call x1, Pallas kernels, step(): pl.pallas_call(step_kernel, out_shape=(jax.ShapeDtypeStruct((EVENTS, D),...  114 us

profile of v4, /device:TPU:0, one launch (start us, length us, event | category | flops | bytes accessed | tf_op | source)
XLA Modules:
  0.0 119.1 jit_solution(14277951894890726434)
XLA Ops:
  0.6 1.3 %broadcast_in_dim.6.gain_ref = f32[1,768]{1,0:T(1,128)} reshape(f32[768]{0:T(1024)} %param.17) | data formatting | bytes 6144 | tf_op jit(solution)/shard_map/broadcast_in_dim | solution.py:806
  1.9 1.3 %pad_add_fusion.lab_ref = s32[4,256]{1,0:T(4,128)} fusion(s32[1,256]{1,0:T(1,128)} %bitcast.8, s32[1,256]{1,0:T(1,128)} %bitcast.9, s32[1,256]{1,0:T(1,128)} %bitcast.10, s32[1,256]{1,0:T(1,128)} %bitcast.11), kind=kLoop, calls=%fused_computation | loop fusion | flops 3072 | bytes 8192 | tf_op jit(solution)/shard_map/concatenate | solution.py:804
  3.2 114.0 %step.1 = (bf16[256,768]{1,0:T(8,128)(2,1)}, f32[8,128]{1,0:T(8,128)}, f32[6,2304]{1,0:T(8,128)}, f32[6,768]{1,0:T(8,128)}, f32[6,1024]{1,0:T(8,128)}, /*index=5*/f32[32,128]{1,0:T(8,128)}) custom-call(bf16[256,768]{1,0:T(8,128)(2,1)} %bitcast.7, s32[4,256]{1,0:T(4,128)} %pad_add_fusion.lab_ref, s32[1,32]{1,0:T(1,128)} %bitcast.12, ...), custom_call_target="tpu_custom_call" | custom-call | tf_op jit(solution)/shard_map/step/pallas_call | solution.py:753
  117.2 1.9 %results.1 = (bf16[256,768]{1,0:T(8,128)(2,1)}, f32[6,2304]{1,0:T(8,128)}, f32[6,768]{1,0:T(8,128)}, f32[6,1024]{1,0:T(8,128)}, f32[32,128]{1,0:T(8,128)}, /*index=5*/f32[6]{0:T(128)}) custom-call(bf16[256,768]{1,0:T(8,128)(2,1)} %get-tuple-element.18.refs_0_, f32[6,2304]{1,0:T(8,128)} %get-tuple-element.19.refs_1_, f32[6,768]{1,0:T(8,128)} %get-tuple-element.20.refs_2_, ...), custom_call_target="tpu_custom_call" | custom-call | tf_op jit(solution)/shard_map/results/pallas_call | solution.py:782

commit v5 on v4

--- a/solution.py
+++ b/solution.py
@@ -97,16 +97,12 @@
 ITEMS = (
     ("t", 128, 128, "zxy"),
     ("p", 48, 512, "yxz"),
-    ("oa", 48, 256, "zxy"),
-    ("ob", 48, 128, "xzy"),
-    ("q0", 48, 128, "xzy"),
-    ("k0", 48, 128, "zxy"),
+    ("o", 48, 384, "zxy"),
+    ("a0", 48, 256, "xzy"),
     ("v0", 48, 128, "yxz"),
-    ("q1", 48, 128, "xzy"),
-    ("k1", 48, 128, "zxy"),
+    ("a1", 48, 256, "zxy"),
     ("v1", 48, 128, "yxz"),
-    ("q2", 48, 128, "xzy"),
-    ("k2", 48, 128, "zxy"),
+    ("a2", 48, 256, "xzy"),
     ("v2", 48, 128, "yxz"),
     ("g", 16, 128, "zxy"),
 )
@@ -160,9 +156,9 @@
     tab_recv,
     src_t,
     src_p,
-    src_oa,
-    src_ob,
-    src_qkv,
+    src_o,
+    src_a,
+    src_v,
     src_g,
     perm,
     turned_p,
@@ -254,10 +250,10 @@
 
     wait_rows(packed, landed, there_send, there_recv, me)
 
-    sources = {"t": src_t, "p": src_p, "oa": src_oa, "ob": src_ob, "g": src_g}
+    sources = {"t": src_t, "p": src_p, "o": src_o, "g": src_g}
     for s in range(3):
-        for part in range(3):
-            sources["qkv"[part] + str(s)] = src_qkv.at[s, part]
+        sources["a%d" % s] = src_a.at[s]
+        sources["v%d" % s] = src_v.at[s]
     mine_at = {"x": x_at, "y": y, "z": z_at}
 
     def place_of(axis, k):
@@ -421,10 +417,11 @@
             for u in range(width // 128):
                 if name == "p":
                     dst, at = piece_ref, u * 256
-                elif name[0] == "o":
-                    dst, at = out_ref, u * 256 if name == "oa" else 512
+                elif name == "o":
+                    dst, at = out_ref, u * 256
                 else:
-                    dst, at = qkv_ref, "qkv".index(name[0]) * D + int(name[1]) * 256
+                    part = u if name[0] == "a" else 2
+                    dst, at = qkv_ref, part * D + int(name[1]) * 256
                 us = slice(u * 128, u * 128 + 128)
                 dst[:, at : at + 128] = total[:6, us]
                 dst[:, at + 128 : at + 256] = total[8:14, us]
@@ -575,20 +572,14 @@
     ctx_t = ctx[...].T
     for j in range(3):
         cols = slice(j * 256, j * 256 + 256)
-        res = stack_halves(mm(ctx_t, ghid[:, cols]))
-        if j < 2:
-            src_oa[:, :, j * 128 : j * 128 + 128] = res
-        else:
-            src_ob[...] = res
-    begin("oa")
-    begin("ob")
+        src_o[:, :, j * 128 : j * 128 + 128] = stack_halves(mm(ctx_t, ghid[:, cols]))
+    begin("o")
     to_first_ring("p")
 
     for j in range(3):
         cols = slice(j * 256, j * 256 + 256)
         gctx[:, cols] = mm_nt(ghid[...], wout[cols, :]).astype(BF16)
-    to_first_ring("oa")
-    to_first_ring("ob")
+    to_first_ring("o")
     normed_t[...] = normed[...].T
     turned_p[...] = mm_nt(perm[...], normed[...]).astype(BF16)
     to_second_ring("t")
@@ -623,11 +614,16 @@
         for part in (2, 0, 1):
             cols = slice(part * D + s * 256, part * D + s * 256 + 256)
             left = turned_p if part == 2 else normed_t
-            src_qkv[s, part] = stack_halves(mm(left[...], dqkv[:, cols]))
-            begin("qkv"[part] + str(s))
+            res = stack_halves(mm(left[...], dqkv[:, cols]))
+            if part == 2:
+                src_v[s] = res
+                begin("v%d" % s)
+            else:
+                src_a[s, :, :, part * 128 : part * 128 + 128] = res
+        begin("a%d" % s)
 
     def each(stage, s):
-        for part in "vqk":
+        for part in "va":
             stage(part + str(s))
 
     backward_step(0)
@@ -640,8 +636,7 @@
     each(to_first_ring, 1)
     qkv_step(2)
     to_second_ring("p")
-    to_second_ring("oa")
-    to_second_ring("ob")
+    to_second_ring("o")
 
     for j in range(3):
         cols = slice(j * 256, j * 256 + 256)
@@ -670,8 +665,7 @@
     each(to_second_ring, 0)
     exchange_rows(rows_out, returned, back_send, back_recv, me, 12, 22)
     to_last("p")
-    to_last("oa")
-    to_last("ob")
+    to_last("o")
     each(to_second_ring, 1)
     exchange_rows(rows_out, returned, back_send, back_recv, me, 22, WIN)
     returned[me] = rows_out[me]
@@ -680,7 +674,7 @@
     each(to_second_ring, 2)
     each(to_last, 1)
     to_last("g")
-    for name in ("t", "p", "oa", "ob"):
+    for name in ("t", "p", "o"):
         finish(name)
     each(finish, 0)
     each(to_last, 2)
@@ -714,9 +708,9 @@
         pltpu.SemaphoreType.DMA((4, 4)),
         pltpu.VMEM((WIN, 128, 128), BF16),
         pltpu.VMEM((WIN, 48, 512), BF16),
-        pltpu.VMEM((WIN, 48, 256), BF16),
-        pltpu.VMEM((WIN, 48, 128), BF16),
-        pltpu.VMEM((3, 3, WIN, 48, 128), BF16),
+        pltpu.VMEM((WIN, 48, 384), BF16),
+        pltpu.VMEM((3, WIN, 48, 256), BF16),
+        pltpu.VMEM((3, WIN, 48, 128), BF16),
         pltpu.VMEM((WIN, SLOT, 128), BF16),
         pltpu.VMEM((D, D), BF16),
         pltpu.VMEM((D, ROWS), BF16),

time: 119 us -> 118 us (level)
  Pallas kernels: 116 us -> 114 us
    pallas_call x1, Pallas kernels: 114 us -> 112 us  [step(): pl.pallas_call(step_kernel, out_shape=(jax.ShapeDtypeStruct((EVENTS, D),...]
where the time goes in v5:
time: 118 us; the launch traced here: 117 us
  Pallas kernels  114 us (97%)
  other arithmetic  1.33 us (1%)
  local copies, waits for them, and re-layouts  1.27 us (1%)
    pallas_call x1, Pallas kernels, step(): pl.pallas_call(step_kernel, out_shape=(jax.ShapeDtypeStruct((EVENTS, D),...  112 us

profile of v5, /device:TPU:0, one launch (start us, length us, event | category | flops | bytes accessed | tf_op | source)
XLA Modules:
  0.0 117.4 jit_solution(2419587106799444973)
XLA Ops:
  0.6 1.3 %broadcast_in_dim.6.gain_ref = f32[1,768]{1,0:T(1,128)} reshape(f32[768]{0:T(1024)} %param.17) | data formatting | bytes 6144 | tf_op jit(solution)/shard_map/broadcast_in_dim | solution.py:800
  1.9 1.3 %pad_add_fusion.lab_ref = s32[4,256]{1,0:T(4,128)} fusion(s32[1,256]{1,0:T(1,128)} %bitcast.8, s32[1,256]{1,0:T(1,128)} %bitcast.9, s32[1,256]{1,0:T(1,128)} %bitcast.10, s32[1,256]{1,0:T(1,128)} %bitcast.11), kind=kLoop, calls=%fused_computation | loop fusion | flops 3072 | bytes 8192 | tf_op jit(solution)/shard_map/concatenate | solution.py:798
  3.2 112.3 %step.1 = (bf16[256,768]{1,0:T(8,128)(2,1)}, f32[8,128]{1,0:T(8,128)}, f32[6,2304]{1,0:T(8,128)}, f32[6,768]{1,0:T(8,128)}, f32[6,1024]{1,0:T(8,128)}, /*index=5*/f32[32,128]{1,0:T(8,128)}) custom-call(bf16[256,768]{1,0:T(8,128)(2,1)} %bitcast.7, s32[4,256]{1,0:T(4,128)} %pad_add_fusion.lab_ref, s32[1,32]{1,0:T(1,128)} %bitcast.12, ...), custom_call_target="tpu_custom_call" | custom-call | tf_op jit(solution)/shard_map/step/pallas_call | solution.py:747
  115.6 1.9 %results.1 = (bf16[256,768]{1,0:T(8,128)(2,1)}, f32[6,2304]{1,0:T(8,128)}, f32[6,768]{1,0:T(8,128)}, f32[6,1024]{1,0:T(8,128)}, f32[32,128]{1,0:T(8,128)}, /*index=5*/f32[6]{0:T(128)}) custom-call(bf16[256,768]{1,0:T(8,128)(2,1)} %get-tuple-element.18.refs_0_, f32[6,2304]{1,0:T(8,128)} %get-tuple-element.19.refs_1_, f32[6,768]{1,0:T(8,128)} %get-tuple-element.20.refs_2_, ...), custom_call_target="tpu_custom_call" | custom-call | tf_op jit(solution)/shard_map/results/pallas_call | solution.py:776

commit v6 on v5

--- a/solution.py
+++ b/solution.py
@@ -655,19 +655,18 @@
     src_g[...] = mm(spread, pick).astype(BF16).reshape(WIN, SLOT, 128)
     begin("g")
     each(to_first_ring, 2)
+    each(to_second_ring, 0)
 
     gh = gn * gain
     gx = inv_rms * (gh - x_hat * jnp.mean(gh * x_hat, -1, keepdims=True))
     gb = (gx + ghid[...].astype(F32)).astype(BF16)
     rows_out[...] = gb.reshape(WIN, SLOT, D)
-    to_first_ring("g")
-    exchange_rows(rows_out, returned, back_send, back_recv, me, 1, 12)
-    each(to_second_ring, 0)
-    exchange_rows(rows_out, returned, back_send, back_recv, me, 12, 22)
     to_last("p")
     to_last("o")
+    to_first_ring("g")
+    exchange_rows(rows_out, returned, back_send, back_recv, me, 1, 16)
     each(to_second_ring, 1)
-    exchange_rows(rows_out, returned, back_send, back_recv, me, 22, WIN)
+    exchange_rows(rows_out, returned, back_send, back_recv, me, 16, WIN)
     returned[me] = rows_out[me]
     to_second_ring("g")
     each(to_last, 0)

time: 118 us -> 117 us (level)
  no operation moved by 1% of the time
where the time goes in v6:
time: 117 us
  Pallas kernels  113 us (97%)
  other arithmetic  1.33 us (1%)
  local copies, waits for them, and re-layouts  1.27 us (1%)
    pallas_call x1, Pallas kernels, step(): pl.pallas_call(step_kernel, out_shape=(jax.ShapeDtypeStruct((EVENTS, D),...  112 us

profile of v6, /device:TPU:0, one launch (start us, length us, event | category | flops | bytes accessed | tf_op | source)
XLA Modules:
  0.0 116.6 jit_solution(10320029061909667050)
XLA Ops:
  0.6 1.3 %broadcast_in_dim.6.gain_ref = f32[1,768]{1,0:T(1,128)} reshape(f32[768]{0:T(1024)} %param.17) | data formatting | bytes 6144 | tf_op jit(solution)/shard_map/broadcast_in_dim | solution.py:799
  1.9 1.3 %pad_add_fusion.lab_ref = s32[4,256]{1,0:T(4,128)} fusion(s32[1,256]{1,0:T(1,128)} %bitcast.8, s32[1,256]{1,0:T(1,128)} %bitcast.9, s32[1,256]{1,0:T(1,128)} %bitcast.10, s32[1,256]{1,0:T(1,128)} %bitcast.11), kind=kLoop, calls=%fused_computation | loop fusion | flops 3072 | bytes 8192 | tf_op jit(solution)/shard_map/concatenate | solution.py:797
  3.2 111.5 %step.1 = (bf16[256,768]{1,0:T(8,128)(2,1)}, f32[8,128]{1,0:T(8,128)}, f32[6,2304]{1,0:T(8,128)}, f32[6,768]{1,0:T(8,128)}, f32[6,1024]{1,0:T(8,128)}, /*index=5*/f32[32,128]{1,0:T(8,128)}) custom-call(bf16[256,768]{1,0:T(8,128)(2,1)} %bitcast.7, s32[4,256]{1,0:T(4,128)} %pad_add_fusion.lab_ref, s32[1,32]{1,0:T(1,128)} %bitcast.12, ...), custom_call_target="tpu_custom_call" | custom-call | tf_op jit(solution)/shard_map/step/pallas_call | solution.py:746
  114.8 1.9 %results.1 = (bf16[256,768]{1,0:T(8,128)(2,1)}, f32[6,2304]{1,0:T(8,128)}, f32[6,768]{1,0:T(8,128)}, f32[6,1024]{1,0:T(8,128)}, f32[32,128]{1,0:T(8,128)}, /*index=5*/f32[6]{0:T(128)}) custom-call(bf16[256,768]{1,0:T(8,128)(2,1)} %get-tuple-element.18.refs_0_, f32[6,2304]{1,0:T(8,128)} %get-tuple-element.19.refs_1_, f32[6,768]{1,0:T(8,128)} %get-tuple-element.20.refs_2_, ...), custom_call_target="tpu_custom_call" | custom-call | tf_op jit(solution)/shard_map/results/pallas_call | solution.py:775
